TPU v7x, 32 devices: a whole 2x2x4 slice. The times are simulated.
32 devices in a mesh: head: 2 (over x), seq: 16 (over z, y, core).
Axes of the slice: x: 2, y: 2, z: 4, core: 2. Of those that a mesh axis runs over, the one named last changes fastest.
Arguments:
- inputs: bfloat16 [2, 4096, 768], P(None, ('seq', 'head')), may hold values from -6 to 6
- cotangent: bfloat16 [2, 4096, 768], P(None, ('seq', 'head')), may hold values from -6 to 6
- lengths: int32 [2, 1, 8], replicated, may hold values from 1 to 1024, 4096 in all within a row
- qkv_weight: float32 [2, 768, 2304], P(None, ('head', 'seq')), may hold values from -0.21875 to 0.21875
- qkv_first: float32 [2, 768, 2304], P(None, ('head', 'seq')), may hold values from -160 to 160
- qkv_second: float32 [2, 768, 2304], P(None, ('head', 'seq')), may hold values from 409.6 to 3276.8
- out_weight: float32 [2, 768, 768], P(None, ('head', 'seq')), may hold values from -0.875 to 0.875
- out_first: float32 [2, 768, 768], P(None, ('head', 'seq')), may hold values from -160 to 160
- out_second: float32 [2, 768, 768], P(None, ('head', 'seq')), may hold values from 409.6 to 3276.8
- up_weight: float32 [2, 768, 6144], P(None, ('head', 'seq')), may hold values from -0.21875 to 0.21875
- up_first: float32 [2, 768, 6144], P(None, ('head', 'seq')), may hold values from -160 to 160
- up_second: float32 [2, 768, 6144], P(None, ('head', 'seq')), may hold values from 409.6 to 3276.8
- down_weight: float32 [2, 3072, 768], P(None, ('head', 'seq')), may hold values from -0.109375 to 0.109375
- down_first: float32 [2, 3072, 768], P(None, ('head', 'seq')), may hold values from -160 to 160
- down_second: float32 [2, 3072, 768], P(None, ('head', 'seq')), may hold values from 409.6 to 3276.8
- norm_params: float32 [2, 768, 4], P(None, ('head', 'seq')), may hold values from -1.2 to 1.65, as said below
- norm_first: float32 [2, 768, 4], P(None, ('head', 'seq')), may hold values from -512 to 512
- norm_second: float32 [2, 768, 4], P(None, ('head', 'seq')), may hold values from 8192 to 32768
Outputs:
- outputs: float32 [2, 4096, 768], P(None, ('seq', 'head'))
- input_grad: float32 [2, 4096, 768], P(None, ('seq', 'head'))
- qkv_grad: float32 [2, 768, 2304], P(None, ('head', 'seq'))
- qkv_first_new: float32 [2, 768, 2304], P(None, ('head', 'seq'))
- qkv_second_new: float32 [2, 768, 2304], P(None, ('head', 'seq'))
- qkv_weight_new: float32 [2, 768, 2304], P(None, ('head', 'seq'))
- out_grad: float32 [2, 768, 768], P(None, ('head', 'seq'))
- out_first_new: float32 [2, 768, 768], P(None, ('head', 'seq'))
- out_second_new: float32 [2, 768, 768], P(None, ('head', 'seq'))
- out_weight_new: float32 [2, 768, 768], P(None, ('head', 'seq'))
- up_grad: float32 [2, 768, 6144], P(None, ('head', 'seq'))
- up_first_new: float32 [2, 768, 6144], P(None, ('head', 'seq'))
- up_second_new: float32 [2, 768, 6144], P(None, ('head', 'seq'))
- up_weight_new: float32 [2, 768, 6144], P(None, ('head', 'seq'))
- down_grad: float32 [2, 3072, 768], P(None, ('head', 'seq'))
- down_first_new: float32 [2, 3072, 768], P(None, ('head', 'seq'))
- down_second_new: float32 [2, 3072, 768], P(None, ('head', 'seq'))
- down_weight_new: float32 [2, 3072, 768], P(None, ('head', 'seq'))
- norm_grad: float32 [2, 768, 4], P(None, ('head', 'seq'))
- norm_first_new: float32 [2, 768, 4], P(None, ('head', 'seq'))
- norm_second_new: float32 [2, 768, 4], P(None, ('head', 'seq'))
- norm_params_new: float32 [2, 768, 4], P(None, ('head', 'seq'))
- qkv_copy: bfloat16 [2, 768, 2304], P(None, ('head', 'seq'))
- out_copy: bfloat16 [2, 768, 768], P(None, ('head', 'seq'))
- up_copy: bfloat16 [2, 768, 6144], P(None, ('head', 'seq'))
- down_copy: bfloat16 [2, 3072, 768], P(None, ('head', 'seq'))
Inputs may be any that keep to these rules, and one draw needn't show every extreme that they name: Each row of 8 lengths sums to 4096, and its largest entry is 1024. `norm_params`: columns 0 and 2 are positive gains, columns 1 and 3 shifts of both signs.
All inputs are finite; a program needn't handle non-finite values.
Results may differ from a plain program's by a relative error of at most 0.03.
The roundings to bfloat16 on the way count: a program that leaves them out, or rounds other values in their place, can miss the bound.
Values may be sent and summed in bfloat16 or wider, within the bound.
A program may use at most 248 MiB of HBM per device.

v0:
```python
import math

import jax
import jax.numpy as jnp
from jax import lax
from jax.sharding import PartitionSpec as P

D = 768
HEADS = 12
HEAD_DIM = 64
FF = 3072
LAYERS = 2
WINDOW = 1024
STEP = 10


beta_one = 0.5
beta_two = 0.5
adam_eps = 1e-08
decay = 0.1
learn_rates = (0.03, 0.15, 0.03, 0.02, 0.2)


def shifted(value, axis, steps):
    count = lax.axis_size(axis)
    first, last = (max(0, -steps), min(count, count - steps))
    return lax.ppermute(value, axis, [(source, source + steps) for source in range(first, last)])


def layer_norm(summed, gain, shift):
    centre = jnp.mean(summed, axis=-1, keepdims=True)
    centred = summed - centre
    variance = jnp.mean(centred * centred, axis=-1, keepdims=True)
    return centred * lax.rsqrt(variance + 1e-12) * gain + shift


def geglu(gate, upper):
    return jax.nn.gelu(gate, approximate=False) * upper


def doc_index(positions, ends):
    return jnp.sum((positions[:, None] >= ends[None, :]).astype(jnp.int32), axis=1)


def batch_context(lengths_row, row_count, reach):
    seq_index = lax.axis_index("seq")
    total_rows = row_count * lax.axis_size("seq")
    seq_count = lengths_row.shape[0]
    seq_tokens = total_rows // seq_count
    seq_starts = jnp.arange(seq_count, dtype=jnp.int32)[:, None] * seq_tokens
    ends = (jnp.cumsum(lengths_row, axis=1) + seq_starts).reshape(-1)
    q_pos = seq_index * row_count + jnp.arange(row_count, dtype=jnp.int32)
    k_pos = (seq_index - reach) * row_count + jnp.arange(
        (2 * reach + 1) * row_count, dtype=jnp.int32
    )
    inside = (k_pos >= 0) & (k_pos < total_rows)
    q_doc = doc_index(q_pos, ends)
    k_doc = jnp.where(inside, doc_index(k_pos, ends), -1)
    return (q_pos, k_pos, q_doc, k_doc)


def block_scores(q_part, k_part, q_pos, k_pos, q_doc, k_doc, slopes):
    raw = jnp.einsum("qhd,khd->hqk", q_part, k_part, preferred_element_type=jnp.float32)
    distance = jnp.abs(q_pos[:, None] - k_pos[None, :])
    allowed = (q_doc[:, None] == k_doc[None, :]) & (distance < WINDOW)
    score = raw * HEAD_DIM ** (-0.5) - slopes[:, None, None] * distance.astype(jnp.float32)[None]
    return jnp.where(allowed[None], score, -1e30)


def block_slices(query, wide_kv, context):
    return (query, wide_kv, context[0], context[1], context[2], context[3])


def attend_forward(query, wide_kv, context):
    slopes, reach = (context[4], context[5])
    row_count = query.shape[0]
    q_block = math.gcd(row_count, 512)

    def forward_block(index):
        q_part, kv_part, q_pos, k_pos, q_doc, k_doc = block_slices(query, wide_kv, context)
        score = block_scores(q_part, kv_part[:, 0], q_pos, k_pos, q_doc, k_doc, slopes)
        top_score = jnp.max(score, axis=-1, keepdims=True)
        log_sum = top_score + jnp.log(jnp.sum(jnp.exp(score - top_score), axis=-1, keepdims=True))
        probs_low = jnp.exp(score - log_sum).astype(jnp.bfloat16)
        attended = jnp.einsum(
            "hqk,khd->qhd", probs_low, kv_part[:, 1], preferred_element_type=jnp.float32
        )
        return (attended, log_sum[..., 0])

    attended, log_sums = lax.map(forward_block, jnp.arange(row_count // q_block, dtype=jnp.int32))
    return (attended.reshape(query.shape), log_sums)


def attend_backward(query, wide_kv, grad_attended, log_sums, context):
    slopes, reach = (context[4], context[5])
    row_count = query.shape[0]
    q_block = math.gcd(row_count, 512)

    def backward_block(grad_wide, index):
        q_part, kv_part, q_pos, k_pos, q_doc, k_doc = block_slices(query, wide_kv, context)
        score = block_scores(q_part, kv_part[:, 0], q_pos, k_pos, q_doc, k_doc, slopes)
        attn_probs = jnp.exp(score - log_sums[index][..., None])
        probs_low = attn_probs.astype(jnp.bfloat16)
        grad_probs = jnp.einsum(
            "qhd,khd->hqk", grad_attended, kv_part[:, 1], preferred_element_type=jnp.float32
        )
        row_dot = jnp.sum(attn_probs * grad_probs, axis=-1, keepdims=True)
        grad_raw = (attn_probs * (grad_probs - row_dot) * HEAD_DIM ** (-0.5)).astype(jnp.bfloat16)
        grad_query = jnp.einsum(
            "hqk,khd->qhd", grad_raw, kv_part[:, 0], preferred_element_type=jnp.float32
        )
        grad_keys = jnp.einsum("hqk,qhd->khd", grad_raw, q_part, preferred_element_type=jnp.float32)
        grad_values = jnp.einsum(
            "hqk,qhd->khd", probs_low, grad_attended, preferred_element_type=jnp.float32
        )
        updated = grad_wide + jnp.stack([grad_keys, grad_values], axis=1)
        return (updated, grad_query)

    zeros_wide = jnp.zeros(wide_kv.shape, jnp.float32)
    grad_wide, grad_queries = lax.scan(
        backward_block, zeros_wide, jnp.arange(row_count // q_block, dtype=jnp.int32)
    )
    return (grad_queries.reshape(query.shape), grad_wide)


def layer_forward(hidden, weights, context):
    qkv_w, out_w, up_w, down_w, norm_w = weights
    heads = lax.axis_size("head")
    tok_rows = hidden.shape[0]
    local_width = D // heads
    local_heads = HEADS // heads
    reach = context[5]
    norm_f = norm_w.astype(jnp.float32)
    hidden_low = hidden.astype(jnp.bfloat16)
    packed = jnp.dot(hidden_low, qkv_w, preferred_element_type=jnp.float32).astype(jnp.bfloat16)
    spread = lax.all_to_all(
        packed.reshape(tok_rows, 3, heads, local_width),
        "head",
        split_axis=2,
        concat_axis=0,
        tiled=True,
    )
    row_count = spread.shape[0]
    query = spread[:, 0, 0].reshape(row_count, local_heads, HEAD_DIM)
    own_kv = spread[:, 1:, 0]
    offsets = list(range(reach, 0, -1)) + list(range(-1, -reach - 1, -1))
    pieces = [shifted(own_kv, "seq", offset) for offset in offsets]
    wide_kv = jnp.concatenate(pieces[:reach] + [own_kv] + pieces[reach:], axis=0)
    wide_kv = wide_kv.reshape(wide_kv.shape[0], 2, local_heads, HEAD_DIM)
    attended, log_sums = attend_forward(query, wide_kv, context)
    attn_heads = attended.astype(jnp.bfloat16).reshape(row_count, 1, local_width)
    attn_low = lax.all_to_all(attn_heads, "head", split_axis=0, concat_axis=1, tiled=True).reshape(
        tok_rows, D
    )
    mixed = hidden + jnp.dot(attn_low, out_w, preferred_element_type=jnp.float32)
    normed = layer_norm(mixed, norm_f[:, 0], norm_f[:, 1])
    normed_low = normed.astype(jnp.bfloat16)
    upper = jnp.dot(normed_low, up_w, preferred_element_type=jnp.float32)
    act_low = geglu(upper[:, :FF], upper[:, FF:]).astype(jnp.bfloat16)
    second = normed + jnp.dot(act_low, down_w, preferred_element_type=jnp.float32)
    result = layer_norm(second, norm_f[:, 2], norm_f[:, 3])
    kept = (
        hidden_low,
        query,
        wide_kv,
        log_sums,
        attn_low,
        mixed,
        normed,
        normed_low,
        upper,
        act_low,
        second,
    )
    return (result, kept)


def layer_backward(grad_result, weights, kept, context):
    qkv_w, out_w, up_w, down_w, norm_w = weights
    (
        hidden_low,
        query,
        wide_kv,
        log_sums,
        attn_low,
        mixed,
        normed,
        normed_low,
        upper,
        act_low,
        second,
    ) = kept
    heads = lax.axis_size("head")
    tok_rows = grad_result.shape[0]
    row_count = query.shape[0]
    local_width = D // heads
    reach = context[5]
    norm_f = norm_w.astype(jnp.float32)
    pull_two = jax.vjp(layer_norm, second, norm_f[:, 2], norm_f[:, 3])[1]
    grad_second, grad_gain_two, grad_shift_two = pull_two(grad_result)
    grad_branch = grad_second.astype(jnp.bfloat16)
    grad_down = jnp.einsum("tf,td->fd", act_low, grad_branch, preferred_element_type=jnp.float32)
    grad_act = jnp.einsum("td,fd->tf", grad_branch, down_w, preferred_element_type=jnp.float32)
    pull_gate = jax.vjp(geglu, upper[:, :FF], upper[:, FF:])[1]
    grad_gate, grad_upper = pull_gate(grad_act)
    grad_up_low = jnp.concatenate([grad_gate, grad_upper], axis=1).astype(jnp.bfloat16)
    grad_up = jnp.einsum("td,tf->df", normed_low, grad_up_low, preferred_element_type=jnp.float32)
    grad_normed = grad_second + jnp.einsum(
        "tf,df->td", grad_up_low, up_w, preferred_element_type=jnp.float32
    )
    pull_one = jax.vjp(layer_norm, mixed, norm_f[:, 0], norm_f[:, 1])[1]
    grad_mixed, grad_gain_one, grad_shift_one = pull_one(grad_normed)
    grad_attn = grad_mixed.astype(jnp.bfloat16)
    grad_out = jnp.einsum("td,te->de", attn_low, grad_attn, preferred_element_type=jnp.float32)
    grad_heads_low = jnp.einsum(
        "te,de->td", grad_attn, out_w, preferred_element_type=jnp.float32
    ).astype(jnp.bfloat16)
    grad_spread = lax.all_to_all(
        grad_heads_low.reshape(tok_rows, heads, local_width),
        "head",
        split_axis=1,
        concat_axis=0,
        tiled=True,
    )
    grad_attended = grad_spread.reshape(query.shape)
    grad_query, grad_wide = attend_backward(query, wide_kv, grad_attended, log_sums, context)
    grad_wide = grad_wide.reshape(grad_wide.shape[0], 2, local_width)
    grad_kv = grad_wide[reach * row_count : (reach + 1) * row_count]
    for distance in range(1, reach + 1):
        for direction in (1, -1):
            block_index = reach - direction * distance
            returned = grad_wide[block_index * row_count : (block_index + 1) * row_count]
            grad_kv = grad_kv + shifted(
                returned.astype(jnp.bfloat16), "seq", -direction * distance
            ).astype(returned.dtype)
    grad_packed = jnp.concatenate([grad_query.reshape(row_count, 1, local_width), grad_kv], axis=1)
    grad_packed = grad_packed.astype(jnp.bfloat16).reshape(row_count, 3, 1, local_width)
    grad_qkv_low = lax.all_to_all(
        grad_packed, "head", split_axis=0, concat_axis=2, tiled=True
    ).reshape(tok_rows, 3 * D)
    grad_qkv = jnp.einsum("td,te->de", hidden_low, grad_qkv_low, preferred_element_type=jnp.float32)
    grad_hidden = grad_mixed + jnp.einsum(
        "te,de->td", grad_qkv_low, qkv_w, preferred_element_type=jnp.float32
    )
    grad_norm = jnp.stack([grad_gain_one, grad_shift_one, grad_gain_two, grad_shift_two], axis=1)
    return (grad_hidden, (grad_qkv, grad_out, grad_up, grad_down, grad_norm))


def adamw(weight, first, second, grad, rate):
    first_new = beta_one * first + (1.0 - beta_one) * grad
    second_new = beta_two * second + (1.0 - beta_two) * grad * grad
    first_hat = first_new / (1.0 - beta_one**STEP)
    second_hat = second_new / (1.0 - beta_two**STEP)
    weight_new = weight - rate * (first_hat / (jnp.sqrt(second_hat) + adam_eps) + decay * weight)
    return (first_new, second_new, weight_new)


def body(
    inputs,
    cotangent,
    lengths,
    qkv_weight,
    qkv_first,
    qkv_second,
    out_weight,
    out_first,
    out_second,
    up_weight,
    up_first,
    up_second,
    down_weight,
    down_first,
    down_second,
    norm_params,
    norm_first,
    norm_second,
):
    masters = (qkv_weight, out_weight, up_weight, down_weight, norm_params)
    states = (
        (qkv_first, qkv_second),
        (out_first, out_second),
        (up_first, up_second),
        (down_first, down_second),
        (norm_first, norm_second),
    )
    heads = lax.axis_size("head")
    sharers = heads * lax.axis_size("seq")
    local_heads = HEADS // heads
    tok_rows = inputs.shape[1]
    row_count = tok_rows * heads
    reach = -(-WINDOW // row_count)
    head_ids = lax.axis_index("head") * local_heads + jnp.arange(local_heads, dtype=jnp.int32)
    slopes = jnp.exp2(-8.0 * (head_ids + 1).astype(jnp.float32) / HEADS)
    qkv_low = qkv_weight.astype(jnp.bfloat16)
    out_low = out_weight.astype(jnp.bfloat16)
    up_low = up_weight.astype(jnp.bfloat16)
    down_low = down_weight.astype(jnp.bfloat16)
    norm_low = norm_params.astype(jnp.bfloat16)
    totals = tuple(
        (
            jnp.zeros((member.shape[0], member.shape[1] * sharers) + member.shape[2:], jnp.float32)
            for member in masters
        )
    )
    outputs_list = []
    input_grads = []
    for batch_index in range(inputs.shape[0]):
        gathered = (
            lax.all_gather(qkv_low, ("head", "seq"), axis=1, tiled=True),
            lax.all_gather(out_low, ("head", "seq"), axis=1, tiled=True),
            lax.all_gather(up_low, ("head", "seq"), axis=1, tiled=True),
            lax.all_gather(down_low, ("head", "seq"), axis=1, tiled=True),
            lax.all_gather(norm_low, ("head", "seq"), axis=1, tiled=True),
        )
        context = batch_context(lengths[batch_index], row_count, reach) + (slopes, reach)
        hidden = inputs[batch_index].astype(jnp.float32)
        kept_all = []
        for layer_index in range(LAYERS):
            layer_weights = tuple((member[layer_index] for member in gathered))
            hidden, kept = layer_forward(hidden, layer_weights, context)
            kept_all.append(kept)
        outputs_list.append(hidden)
        grad_hidden = cotangent[batch_index].astype(jnp.float32)
        layer_grads = [None] * LAYERS
        for layer_index in reversed(range(LAYERS)):
            layer_weights = tuple((member[layer_index] for member in gathered))
            grad_hidden, layer_grads[layer_index] = layer_backward(
                grad_hidden, layer_weights, kept_all[layer_index], context
            )
        input_grads.append(grad_hidden)
        full_grads = tuple(
            (
                jnp.stack([layer_grads[layer_index][kind_index] for layer_index in range(LAYERS)])
                for kind_index in range(5)
            )
        )
        totals = tuple((total + piece for total, piece in zip(totals, full_grads)))
    totals = (
        lax.psum_scatter(totals[0], ("head", "seq"), scatter_dimension=1, tiled=True),
        lax.psum_scatter(totals[1], ("head", "seq"), scatter_dimension=1, tiled=True),
        lax.psum_scatter(totals[2], ("head", "seq"), scatter_dimension=1, tiled=True),
        lax.psum_scatter(totals[3], ("head", "seq"), scatter_dimension=1, tiled=True),
        lax.psum_scatter(totals[4], ("head", "seq"), scatter_dimension=1, tiled=True),
    )
    results = [jnp.stack(outputs_list), jnp.stack(input_grads)]
    new_weights = []
    for kind_index in range(5):
        first_new, second_new, weight_new = adamw(
            masters[kind_index],
            states[kind_index][0],
            states[kind_index][1],
            totals[kind_index],
            learn_rates[kind_index],
        )
        results += [totals[kind_index], first_new, second_new, weight_new]
        new_weights.append(weight_new)
    results += [member.astype(jnp.bfloat16) for member in new_weights[:4]]
    return tuple(results)


def solution(mesh):
    in_specs = (
        P(None, ("seq", "head"), None),
        P(None, ("seq", "head"), None),
        P(),
        P(None, ("head", "seq"), None),
        P(None, ("head", "seq"), None),
        P(None, ("head", "seq"), None),
        P(None, ("head", "seq"), None),
        P(None, ("head", "seq"), None),
        P(None, ("head", "seq"), None),
        P(None, ("head", "seq"), None),
        P(None, ("head", "seq"), None),
        P(None, ("head", "seq"), None),
        P(None, ("head", "seq"), None),
        P(None, ("head", "seq"), None),
        P(None, ("head", "seq"), None),
        P(None, ("head", "seq"), None),
        P(None, ("head", "seq"), None),
        P(None, ("head", "seq"), None),
    )
    out_specs = (
        P(None, ("seq", "head"), None),
        P(None, ("seq", "head"), None),
        P(None, ("head", "seq"), None),
        P(None, ("head", "seq"), None),
        P(None, ("head", "seq"), None),
        P(None, ("head", "seq"), None),
        P(None, ("head", "seq"), None),
        P(None, ("head", "seq"), None),
        P(None, ("head", "seq"), None),
        P(None, ("head", "seq"), None),
        P(None, ("head", "seq"), None),
        P(None, ("head", "seq"), None),
        P(None, ("head", "seq"), None),
        P(None, ("head", "seq"), None),
        P(None, ("head", "seq"), None),
        P(None, ("head", "seq"), None),
        P(None, ("head", "seq"), None),
        P(None, ("head", "seq"), None),
        P(None, ("head", "seq"), None),
        P(None, ("head", "seq"), None),
        P(None, ("head", "seq"), None),
        P(None, ("head", "seq"), None),
        P(None, ("head", "seq"), None),
        P(None, ("head", "seq"), None),
        P(None, ("head", "seq"), None),
        P(None, ("head", "seq"), None),
    )
    return jax.shard_map(body, mesh=mesh, in_specs=in_specs, out_specs=out_specs, check_vma=False)
```

profile of v0, /device:TPU:0, one launch (start us, length us, event | category | flops | bytes accessed | tf_op | source)
XLA Modules:
  0.0 2143.7 jit_solution(10901126828347679571)
XLA Ops:
  14.8 72.3 %all-gather.5.cloned.1.call-done = bf16[2,768,2304]{2,1,0:T(8,128)(2,1)} async-done(((bf16[2,24,2304]{2,1,0:T(8,128)(2,1)}), bf16[2,768,2304]{2,1,0:T(8,128)(2,1)}) %all-gather.5.cloned.1.call-update) | async-done | bytes 7077904 | tf_op jit(solution)/shard_map/all_gather | solution.py:309
  121.3 54.5 %all_gather.22 = bf16[2,768,4]{2,0,1:T(2,128)(2,1)S(1)} all-gather(bf16[2,24,4]{2,0,1:T(2,128)(2,1)S(1)} %copy.749), channel_id=1, replica_groups=mesh['head'=2,'seq'=16] {'head','seq'}, dimensions={1}, use_global_device_ids=true | all-gather | bytes 12672 | tf_op jit(solution)/shard_map/all_gather | solution.py:313
  241.8 19.8 collective-permute-done.7
  384.7 26.0 %all-gather.11.cloned.1.call-done = bf16[2,3072,768]{2,1,0:T(8,128)(2,1)} async-done(((bf16[2,96,768]{2,1,0:T(8,128)(2,1)}), bf16[2,3072,768]{2,1,0:T(8,128)(2,1)}) %all-gather.11.cloned.1.call-update) | async-done | bytes 9437200 | tf_op jit(solution)/shard_map/all_gather | solution.py:312
  517.3 10.0 fusion.307
  582.5 10.0 fusion.313
  701.8 24.0 %fusion.172 = bf16[6,64,256]{2,1,0:T(8,128)(2,1)} fusion(f32[6,256,2304]{2,1,0:T(8,128)} %fusion.149, f32[6,256,2304]{2,1,0:T(8,128)} %get-tuple-element.674, f32[6,256]{1,0:T(8,128)S(1)} %copy-done.154, bf16[2304,2,6,64]{0,3,2,1:T(8,128)(2,1)S(1)} %copy-done.20), kind=kOutput, calls=%fused_computation.264 | convolution fusion | flops 477859584 | bytes 58605568 | tf_op jit(solution)/shard_map/while/body/eval_jaxpr/hqk,khd->qhd/dot_general | solution.py:109
  725.7 26.5 %fusion.87 = f32[2304,1,6,64]{0,3,2,1:T(8,128)} fusion(bf16[256,6,64]{0,2,1:T(8,128)(2,1)} %bitcast.671, f32[6,256,2304]{2,1,0:T(8,128)} %fusion.149, f32[6,256,2304]{2,1,0:T(8,128)} %get-tuple-element.674, f32[6,256]{1,0:T(8,128)} %copy-done.153), kind=kOutput, calls=%fused_computation.105 | convolution fusion | flops 477761280 | bytes 32053248 | tf_op jit(solution)/shard_map/while/body/eval_jaxpr/hqk,qhd->khd/dot_general | solution.py:112
  799.0 26.6 %fusion.93 = f32[2304,1,6,64]{0,3,2,1:T(8,128)} fusion(bf16[256,6,64]{0,2,1:T(8,128)(2,1)} %bitcast.669, f32[6,256,2304]{2,1,0:T(8,128)} %fusion.147, f32[6,256,2304]{2,1,0:T(8,128)} %get-tuple-element.662, f32[6,256]{1,0:T(8,128)S(1)} %copy-done.152), kind=kOutput, calls=%fused_computation.107 | convolution fusion | flops 477761280 | bytes 32053248 | tf_op jit(solution)/shard_map/while/body/eval_jaxpr/hqk,qhd->khd/dot_general | solution.py:112
  860.6 10.0 collective-permute-start.39
  879.3 23.6 %fusion.178 = bf16[6,64,256]{2,1,0:T(8,128)(2,1)S(1)} fusion(f32[6,256,2304]{2,1,0:T(8,128)} %fusion.147, f32[6,256,2304]{2,1,0:T(8,128)} %get-tuple-element.662, f32[6,256]{1,0:T(8,128)S(1)} %copy-done.152, bf16[2304,2,6,64]{0,3,2,1:T(8,128)(2,1)} %copy-done.17), kind=kOutput, calls=%fused_computation.266 | convolution fusion | flops 477859584 | bytes 58605568 | tf_op jit(solution)/shard_map/while/body/eval_jaxpr/hqk,khd->qhd/dot_general | solution.py:109
  922.3 11.2 collective-permute-done.35
  1018.3 26.6 %fusion.84 = f32[2304,1,6,64]{0,3,2,1:T(8,128)} fusion(bf16[256,6,64]{0,2,1:T(8,128)(2,1)} %bitcast.666, f32[6,256,2304]{2,1,0:T(8,128)} %fusion.148, f32[6,256,2304]{2,1,0:T(8,128)} %get-tuple-element.668, f32[6,256]{1,0:T(8,128)S(1)} %copy-done.150), kind=kOutput, calls=%fused_computation.104 | convolution fusion | flops 477761280 | bytes 32053248 | tf_op jit(solution)/shard_map/while/body/eval_jaxpr/hqk,qhd->khd/dot_general | solution.py:112
  1095.4 26.5 %fusion.90 = f32[2304,1,6,64]{0,3,2,1:T(8,128)} fusion(bf16[256,6,64]{0,2,1:T(8,128)(2,1)} %bitcast.664, f32[6,256,2304]{2,1,0:T(8,128)} %fusion.146, f32[6,256,2304]{2,1,0:T(8,128)} %get-tuple-element.656, f32[6,256]{1,0:T(8,128)S(1)} %copy-done.148), kind=kOutput, calls=%fused_computation.106 | convolution fusion | flops 477761280 | bytes 32053248 | tf_op jit(solution)/shard_map/while/body/eval_jaxpr/hqk,qhd->khd/dot_general | solution.py:112
  1121.8 23.6 %fusion.169 = bf16[6,64,256]{2,1,0:T(8,128)(2,1)} fusion(f32[6,256,2304]{2,1,0:T(8,128)} %fusion.148, f32[6,256,2304]{2,1,0:T(8,128)} %get-tuple-element.668, f32[6,256]{1,0:T(8,128)} %copy-done.149, bf16[2304,2,6,64]{0,3,2,1:T(8,128)(2,1)S(1)} %copy-done.16), kind=kOutput, calls=%fused_computation.263 | convolution fusion | flops 477859584 | bytes 58605568 | tf_op jit(solution)/shard_map/while/body/eval_jaxpr/hqk,khd->qhd/dot_general | solution.py:109
  1202.3 23.6 %fusion.175 = bf16[6,64,256]{2,1,0:T(8,128)(2,1)S(1)} fusion(f32[6,256,2304]{2,1,0:T(8,128)} %fusion.146, f32[6,256,2304]{2,1,0:T(8,128)} %get-tuple-element.656, f32[6,256]{1,0:T(8,128)S(1)} %copy-done.148, bf16[2304,2,6,64]{0,3,2,1:T(8,128)(2,1)} %copy-done.12), kind=kOutput, calls=%fused_computation.265 | convolution fusion | flops 477859584 | bytes 58605568 | tf_op jit(solution)/shard_map/while/body/eval_jaxpr/hqk,khd->qhd/dot_general | solution.py:109
  1246.4 11.5 collective-permute-done.43
  1291.2 21.6 %copy.854 = f32[2,768,2304]{2,0,1:T(2,128)} copy(f32[2,768,2304]{1,2,0:T(8,128)} %maximum_add_fusion.2) | data formatting | bytes 28311552 | tf_op jit(solution)/shard_map/add | solution.py:337
  1323.7 11.9 maximum_add_fusion.1
  1371.7 38.2 %maximum_add_fusion = f32[2,768,6144]{2,1,0:T(8,128)} fusion(f32[1,768,6144]{2,1,0:T(8,128)} %convolution_bitcast_fusion.2, f32[1,768,6144]{2,1,0:T(8,128)} %convolution_bitcast_fusion.3, f32[1,768,6144]{2,1,0:T(8,128)} %convolution_bitcast_fusion, f32[1,768,6144]{2,1,0:T(8,128)} %convolution_bitcast_fusion.1), kind=kLoop, calls=%fused_computation.4 | loop fusion | flops 28311552 | bytes 113246208 | tf_op jit(solution)/shard_map/add | solution.py:337
  1412.5 47.0 %all-reduce.1 = f32[2,768,4]{1,2,0:T(4,128)S(1)} all-reduce(f32[2,768,4]{1,2,0:T(4,128)S(1)} %maximum_add_fusion.4), channel_id=6, replica_groups=mesh['head'=2,'seq'=16] {'head','seq'}, use_global_device_ids=true, to_apply=%region_70.71.clone | all-reduce | flops 6144 | bytes 49152
  1469.8 96.1 %all-reduce.4.cloned.1.call-done = f32[2,768,2304]{2,0,1:T(2,128)} async-done(((f32[2,768,2304]{2,0,1:T(2,128)}), f32[2,768,2304]{2,0,1:T(2,128)}) %all-reduce.4.cloned.1.call-update) | async-done | bytes 14155792
  1568.3 210.3 %reduce-scatter.9.cloned.1.call-done = f32[2,96,768]{2,1,0:T(8,128)} async-done(((f32[2,3072,768]{2,1,0:T(8,128)}), f32[2,96,768]{2,1,0:T(8,128)}) %reduce-scatter.9.cloned.1.call-update) | async-done | bytes 589840 | tf_op jit(solution)/shard_map/reduce_scatter | solution.py:342
  1781.5 350.6 %reduce-scatter.7.cloned.1.call-done = f32[2,24,6144]{2,1,0:T(8,128)} async-done(((f32[2,768,6144]{2,1,0:T(8,128)}), f32[2,24,6144]{2,1,0:T(8,128)}) %reduce-scatter.7.cloned.1.call-update) | async-done | bytes 1179664 | tf_op jit(solution)/shard_map/reduce_scatter | solution.py:341
  (1069 shorter events, 922.6 us)
Async XLA Ops:
  7.2 79.8 %all-gather.5.cloned.1.call-start = ((), (), s32[]{:S(2)}) async-start(), calls=%async_computation.19 | async-start | bytes 7299072 | tf_op jit(solution)/shard_map/all_gather | solution.py:309
  9.1 360.0 %all-gather.7.cloned.1.call-start = ((), (), s32[]{:S(2)}) async-start(), calls=%async_computation.20 | async-start | bytes 2433024 | tf_op jit(solution)/shard_map/all_gather | solution.py:310
  10.7 362.4 %all-gather.9.cloned.1.call-start = ((), (), s32[]{:S(2)}) async-start(), calls=%async_computation.21 | async-start | bytes 19464192 | tf_op jit(solution)/shard_map/all_gather | solution.py:311
  13.0 397.7 %all-gather.11.cloned.1.call-start = ((), (), s32[]{:S(2)}) async-start(), calls=%async_computation.22 | async-start | bytes 9732096 | tf_op jit(solution)/shard_map/all_gather | solution.py:312
  108.5 81.9 %collective-permute-start = (bf16[256,2,384]{2,0,1:T(8,128)(2,1)}, bf16[256,2,384]{2,0,1:T(8,128)(2,1)}, u32[]{:S(2)}, u32[]{:S(2)}) collective-permute-start(bf16[256,2,384]{2,0,1:T(8,128)(2,1)} %get-tuple-element.624), channel_id=1, source_target_pairs={{0,4},{1,5},{2,6},{3,7},{4,8},{5,9},{6,10},{7,11},{8,12},{9,13},{1... | collective-permute-start | bytes 1179656 | tf_op jit(solution)/shard_map/ppermute | solution.py:27
  112.6 79.1 %collective-permute-start.1 = (bf16[256,2,384]{2,0,1:T(8,128)(2,1)}, bf16[256,2,384]{2,0,1:T(8,128)(2,1)}, u32[]{:S(2)}, u32[]{:S(2)}) collective-permute-start(bf16[256,2,384]{2,0,1:T(8,128)(2,1)} %get-tuple-element.624), channel_id=1, source_target_pairs={{0,3},{1,4},{2,5},{3,6},{4,7},{5,8},{6,9},{7,10},{8,11},{9,12},{10... | collective-permute-start | bytes 1179656 | tf_op jit(solution)/shard_map/ppermute | solution.py:27
  115.6 77.4 %collective-permute-start.2 = (bf16[256,2,384]{2,0,1:T(8,128)(2,1)}, bf16[256,2,384]{2,0,1:T(8,128)(2,1)}, u32[]{:S(2)}, u32[]{:S(2)}) collective-permute-start(bf16[256,2,384]{2,0,1:T(8,128)(2,1)} %get-tuple-element.624), channel_id=1, source_target_pairs={{0,2},{1,3},{2,4},{3,5},{4,6},{5,7},{6,8},{7,9},{8,10},{9,11},{10,... | collective-permute-start | bytes 1179656 | tf_op jit(solution)/shard_map/ppermute | solution.py:27
  214.1 69.9 %collective-permute-start.16 = (bf16[256,2,384]{2,0,1:T(8,128)(2,1)}, bf16[256,2,384]{2,0,1:T(8,128)(2,1)}, u32[]{:S(2)}, u32[]{:S(2)}) collective-permute-start(bf16[256,2,384]{2,0,1:T(8,128)(2,1)} %get-tuple-element.628), channel_id=1, source_target_pairs={{0,4},{1,5},{2,6},{3,7},{4,8},{5,9},{6,10},{7,11},{8,12},{9,13},{1... | collective-permute-start | bytes 1179656 | tf_op jit(solution)/shard_map/ppermute | solution.py:27
  233.5 78.9 %collective-permute-start.19 = (bf16[256,2,384]{2,0,1:T(8,128)(2,1)}, bf16[256,2,384]{2,0,1:T(8,128)(2,1)}, u32[]{:S(2)}, u32[]{:S(2)}) collective-permute-start(bf16[256,2,384]{2,0,1:T(8,128)(2,1)} %get-tuple-element.628), channel_id=1, source_target_pairs={{0,1},{1,2},{2,3},{3,4},{4,5},{5,6},{6,7},{7,8},{8,9},{9,10},{10,1... | collective-permute-start | bytes 1179656 | tf_op jit(solution)/shard_map/ppermute | solution.py:27
  680.3 71.9 %all-to-all-start.8 = ((bf16[128,2,384]{2,0,1:T(8,128)(2,1)}), bf16[128,2,384]{2,0,1:T(8,128)(2,1)}, u32[]{:S(2)}, u32[]{:S(2)}) async-start(bf16[128,2,384]{2,0,1:T(8,128)(2,1)} %bitcast.547), calls=%async_computation.8 | async-start | bytes 393216 | tf_op jit(solution)/shard_map/all_to_all | solution.py:218
  779.7 75.7 %collective-permute-start.54 = (bf16[256,2,384]{2,0,1:T(8,128)(2,1)}, bf16[256,2,384]{2,0,1:T(8,128)(2,1)}, u32[]{:S(2)}, u32[]{:S(2)}) collective-permute-start(bf16[256,2,384]{2,0,1:T(8,128)(2,1)} %copy.831), channel_id=1, source_target_pairs={{4,0},{5,1},{6,2},{7,3},{8,4},{9,5},{10,6},{11,7},{12,8},{13,9},{1... | collective-permute-start | bytes 1179656 | tf_op jit(solution)/shard_map/ppermute | solution.py:27
  782.9 76.4 %collective-permute-start.53 = (bf16[256,2,384]{2,0,1:T(8,128)(2,1)}, bf16[256,2,384]{2,0,1:T(8,128)(2,1)}, u32[]{:S(2)}, u32[]{:S(2)}) collective-permute-start(bf16[256,2,384]{2,0,1:T(8,128)(2,1)} %copy.830), channel_id=1, source_target_pairs={{0,3},{1,4},{2,5},{3,6},{4,7},{5,8},{6,9},{7,10},{8,11},{9,12},{10... | collective-permute-start | bytes 1179656 | tf_op jit(solution)/shard_map/ppermute | solution.py:27
  787.5 73.1 %collective-permute-start.52 = (bf16[256,2,384]{2,0,1:T(8,128)(2,1)}, bf16[256,2,384]{2,0,1:T(8,128)(2,1)}, u32[]{:S(2)}, u32[]{:S(2)}) collective-permute-start(bf16[256,2,384]{2,0,1:T(8,128)(2,1)} %copy.829), channel_id=1, source_target_pairs={{3,0},{4,1},{5,2},{6,3},{7,4},{8,5},{9,6},{10,7},{11,8},{12,9},{13... | collective-permute-start | bytes 1179656 | tf_op jit(solution)/shard_map/ppermute | solution.py:27
  790.7 79.9 %collective-permute-start.51 = (bf16[256,2,384]{2,0,1:T(8,128)(2,1)}, bf16[256,2,384]{2,0,1:T(8,128)(2,1)}, u32[]{:S(2)}, u32[]{:S(2)}) collective-permute-start(bf16[256,2,384]{2,0,1:T(8,128)(2,1)} %copy.828), channel_id=1, source_target_pairs={{0,2},{1,3},{2,4},{3,5},{4,6},{5,7},{6,8},{7,9},{8,10},{9,11},{10,... | collective-permute-start | bytes 1179656 | tf_op jit(solution)/shard_map/ppermute | solution.py:27
  992.0 475.9 %reduce-scatter.5.cloned.1.call-start = ((), (), s32[]{:S(2)}) async-start(), calls=%async_computation.23 | async-start | bytes 4866048 | tf_op jit(solution)/shard_map/reduce_scatter | solution.py:340
  998.5 85.5 %all-to-all-start.10 = ((bf16[128,2,384]{2,0,1:T(8,128)(2,1)}), bf16[128,2,384]{2,0,1:T(8,128)(2,1)}, u32[]{:S(2)}, u32[]{:S(2)}) async-start(bf16[128,2,384]{2,0,1:T(8,128)(2,1)} %bitcast.546), calls=%async_computation.10 | async-start | bytes 393216 | tf_op jit(solution)/shard_map/all_to_all | solution.py:218
  1051.3 104.3 %collective-permute-start.63 = (bf16[256,2,384]{2,0,1:T(8,128)(2,1)}, bf16[256,2,384]{2,0,1:T(8,128)(2,1)}, u32[]{:S(2)}, u32[]{:S(2)}) collective-permute-start(bf16[256,2,384]{2,0,1:T(8,128)(2,1)} %copy.847), channel_id=1, source_target_pairs={{0,4},{1,5},{2,6},{3,7},{4,8},{5,9},{6,10},{7,11},{8,12},{9,13},{1... | collective-permute-start | bytes 1179656 | tf_op jit(solution)/shard_map/ppermute | solution.py:27
  1060.0 121.4 %collective-permute-start.62 = (bf16[256,2,384]{2,0,1:T(8,128)(2,1)}, bf16[256,2,384]{2,0,1:T(8,128)(2,1)}, u32[]{:S(2)}, u32[]{:S(2)}) collective-permute-start(bf16[256,2,384]{2,0,1:T(8,128)(2,1)} %copy.846), channel_id=1, source_target_pairs={{4,0},{5,1},{6,2},{7,3},{8,4},{9,5},{10,6},{11,7},{12,8},{13,9},{1... | collective-permute-start | bytes 1179656 | tf_op jit(solution)/shard_map/ppermute | solution.py:27
  1063.2 122.0 %collective-permute-start.61 = (bf16[256,2,384]{2,0,1:T(8,128)(2,1)}, bf16[256,2,384]{2,0,1:T(8,128)(2,1)}, u32[]{:S(2)}, u32[]{:S(2)}) collective-permute-start(bf16[256,2,384]{2,0,1:T(8,128)(2,1)} %copy.845), channel_id=1, source_target_pairs={{0,3},{1,4},{2,5},{3,6},{4,7},{5,8},{6,9},{7,10},{8,11},{9,12},{10... | collective-permute-start | bytes 1179656 | tf_op jit(solution)/shard_map/ppermute | solution.py:27
  1067.1 119.3 %collective-permute-start.60 = (bf16[256,2,384]{2,0,1:T(8,128)(2,1)}, bf16[256,2,384]{2,0,1:T(8,128)(2,1)}, u32[]{:S(2)}, u32[]{:S(2)}) collective-permute-start(bf16[256,2,384]{2,0,1:T(8,128)(2,1)} %copy.844), channel_id=1, source_target_pairs={{3,0},{4,1},{5,2},{6,3},{7,4},{8,5},{9,6},{10,7},{11,8},{12,9},{13... | collective-permute-start | bytes 1179656 | tf_op jit(solution)/shard_map/ppermute | solution.py:27
  1070.3 122.8 %collective-permute-start.59 = (bf16[256,2,384]{2,0,1:T(8,128)(2,1)}, bf16[256,2,384]{2,0,1:T(8,128)(2,1)}, u32[]{:S(2)}, u32[]{:S(2)}) collective-permute-start(bf16[256,2,384]{2,0,1:T(8,128)(2,1)} %copy.843), channel_id=1, source_target_pairs={{0,2},{1,3},{2,4},{3,5},{4,6},{5,7},{6,8},{7,9},{8,10},{9,11},{10,... | collective-permute-start | bytes 1179656 | tf_op jit(solution)/shard_map/ppermute | solution.py:27
  1265.9 300.0 %all-reduce.4.cloned.1.call-start = ((), (), s32[]{:S(2)}) async-start(), calls=%async_computation.26 | async-start | bytes 28311552
  1312.9 465.8 %reduce-scatter.9.cloned.1.call-start = ((), (), s32[]{:S(2)}) async-start(), calls=%async_computation.25 | async-start | bytes 19464192 | tf_op jit(solution)/shard_map/reduce_scatter | solution.py:342
  1335.6 796.5 %reduce-scatter.7.cloned.1.call-start = ((), (), s32[]{:S(2)}) async-start(), calls=%async_computation.24 | async-start | bytes 38928384 | tf_op jit(solution)/shard_map/reduce_scatter | solution.py:341
  (320 other events, 8172.0 us)
Sparse Core Ops, SparseCore 0:
  11.6 75.4 all-gather.4
  90.6 58.5 all-gather.6
  152.7 164.5 all-gather.8
  320.7 89.9 all-gather.10
  998.6 126.0 reduce-scatter.4
  1313.0 252.8 all-reduce.3
  1574.0 204.6 reduce-scatter.8
  1786.8 345.2 reduce-scatter.6
where the time goes:
time: 2160 us; the launch traced here: 2140 us
  waiting for transfers between devices  842 us (39%)
  matrix products  498 us (23%)
  local copies, waits for them, and re-layouts  273 us (13%)
  starting transfers between devices  245 us (11%)
  other arithmetic  165 us (8%)
  blocking collectives  101 us (5%)
    reduce_scatter x1, waiting for transfers between devices, body(): lax.psum_scatter(totals[2], ('head', 'seq'), scatter_dimension=1, tiled=T...  351 us
    reduce_scatter x1, waiting for transfers between devices, body(): lax.psum_scatter(totals[3], ('head', 'seq'), scatter_dimension=1, tiled=T...  210 us
    ppermute x64, starting transfers between devices, shifted(): lax.ppermute(value, axis, [(source, source + steps) for source in range(f...  182 us
    dot_general x4, matrix products, backward_block(): jnp.einsum('hqk,qhd->khd', grad_raw, q_part, preferred_element_type=jnp.f...  106 us
    unnamed x9, waiting for transfers between devices  96.2 us
    dot_general x4, matrix products, backward_block(): jnp.einsum('hqk,khd->qhd', grad_raw, kv_part[:, 0], preferred_element_typ...  94.8 us
    all_gather x1, waiting for transfers between devices, body(): lax.all_gather(qkv_low, ('head', 'seq'), axis=1, tiled=True)  72.3 us
    ppermute x64, waiting for transfers between devices, shifted(): lax.ppermute(value, axis, [(source, source + steps) for source in range(f...  66.3 us
  transfers between devices with their start and end apart: 88, of which 16 were waited for; matrix products, arithmetic and copies ran while one was open for 38% of the time, Pallas kernels for 0%

commit v1 on v0

v1 whole, which is shorter than its diff:
```python
import functools
import math

import jax
import jax.numpy as jnp
from jax import lax
from jax.experimental import pallas as pl
from jax.experimental.pallas import tpu as pltpu
from jax.sharding import PartitionSpec as P

D = 768
HEADS = 12
HEAD_DIM = 64
FF = 3072
LAYERS = 2
WINDOW = 1024
STEP = 10

beta_one = 0.5
beta_two = 0.5
adam_eps = 1e-08
decay = 0.1
learn_rates = (0.03, 0.15, 0.03, 0.02, 0.2)

MESH = pl.DeviceIdType.MESH
TILE = 256
LOG2E = math.log2(math.e)
NORM_PAD = 128

CORES = 2
AXES = ("x", "z", "y", "c")


def cost_of(microseconds):
    return pl.CostEstimate(flops=0, bytes_accessed=int(microseconds * 3.69e6), transcendentals=0)


def grid_sizes(seq_size):
    rows = 2 if seq_size <= 16 else 4
    return {"x": lax.axis_size("head"), "z": seq_size // (rows * CORES), "y": rows, "c": CORES}


def quotient(value, divisor, count):
    result = 0
    for step in range(1, count):
        result = result + jnp.where(value >= step * divisor, 1, 0)
    return result


def wrapped(value, size):
    return value - jnp.where(value >= size, size, 0)


def own_place(sizes):
    seq = lax.axis_index("seq")
    return {
        "x": lax.axis_index("head"),
        "z": lax.div(seq, sizes["y"] * sizes["c"]),
        "y": lax.rem(lax.div(seq, sizes["c"]), sizes["y"]),
        "c": lax.rem(seq, sizes["c"]),
    }


def device_of(place, sizes):
    seq = (place["z"] * sizes["y"] + place["y"]) * sizes["c"] + place["c"]
    return {"head": place["x"], "seq": seq}


def peer_at(place, axis, step, sizes):
    other = dict(place)
    other[axis] = lax.rem(place[axis] + step, sizes[axis])
    return other


def greet_axes(place, sizes):
    barrier = pltpu.get_barrier_semaphore()
    count = 0
    for axis in AXES:
        for step in range(1, sizes[axis]):
            pl.semaphore_signal(
                barrier,
                inc=1,
                device_id=device_of(peer_at(place, axis, step, sizes), sizes),
                device_id_type=MESH,
            )
            count += 1
    pl.semaphore_wait(barrier, count)


def region(place, full, window):
    return tuple(slice(None) if axis in full else place[axis] for axis in AXES) + window


ZXY = ("z", "x", "y")
ZYX = ("z", "y", "x")

def steps_of(kind, rows):
    def halves(first, second, start=0):
        return ((0, rows, start, first, ZXY), (0, rows, start + first, second, ZYX))

    if kind == "qkv":
        return [halves(384, 384, start) for start in range(0, 3 * D, 768)]
    if kind == "out":
        return [halves(384, 512)]
    if kind == "up":
        return [halves(768, 768, start) for start in range(0, 2 * FF, 1536)]
    if rows % 32:
        return [halves(384, 384)]
    half = rows // 2
    return [
        ((0, half, start, 384, ZXY), (half, half, start, 384, ZYX)) for start in range(0, D, 384)
    ]


HBM = pl.BlockSpec(memory_space=pl.ANY)
VMEM = pl.BlockSpec(memory_space=pltpu.VMEM)
SMEM = pl.BlockSpec(memory_space=pltpu.SMEM)


class Flow:
    def __init__(self, kinds, operands, sizes, ahead, lag):
        self.operands = list(operands)
        self.sizes = sizes
        self.ahead, self.lag = ahead, lag
        self.steps, self.pieces = [], []
        for array, kind in enumerate(kinds):
            for step in steps_of(kind, operands[array].shape[-2]):
                self.steps.append(range(len(self.pieces), len(self.pieces) + len(step)))
                self.pieces += [(array,) + piece for piece in step]
        most = sum(size - 1 for size in sizes.values())
        self.semaphores = [
            pltpu.SemaphoreType.DMA((len(self.pieces), most)),
            pltpu.SemaphoreType.DMA((len(self.pieces), most)),
            pltpu.SemaphoreType.DMA((len(self.pieces),)),
        ]

        if not self.pieces:
            self.ahead, self.semaphores = 0, []

    def bind(self, ins, outs, scratch):
        self.place = own_place(self.sizes)
        if self.pieces:
            self.ins, self.outs, self.buffers = ins, outs, scratch[:-3]
            self.send_sem, self.recv_sem, self.own_sem = scratch[-3:]

    def window(self, number):
        _, row, rows, column, columns, _ = self.pieces[number]
        return (pl.ds(row, rows), pl.ds(column, columns))

    def remote(self, number, axis, step, source, target):
        before = AXES[: AXES.index(axis)]
        slot = sum(self.sizes[one] - 1 for one in before) + step - 1
        return pltpu.make_async_remote_copy(
            src_ref=source,
            dst_ref=target,
            send_sem=self.send_sem.at[number, slot],
            recv_sem=self.recv_sem.at[number, slot],
            device_id=device_of(peer_at(self.place, axis, step, self.sizes), self.sizes),
            device_id_type=MESH,
        )

    def numbers(self, step):
        return self.steps[step] if 0 <= step < len(self.steps) else ()

    def start(self, step, phase):
        for number in self.numbers(step):
            if phase == 0:
                self.own_copy(number).start()
            for copy in self.copies(number, phase):
                copy.start()

    def begin(self):
        for step in range(self.ahead):
            self.start(step, 0)

    def arrive(self, step, phase):
        for number in self.numbers(step):
            if phase == 0:
                self.own_copy(number).wait()
            for copy in self.copies(number, phase):
                copy.wait_recv()
            self.take(number, phase)

    def turns(self):
        def turn(index):
            self.start(index + self.ahead, 0)
            for phase in (3, 2, 1, 0):
                self.arrive(index - self.lag * phase, phase)
                if phase < 3:
                    self.start(index - self.lag * phase, phase + 1)

        count = len(self.steps) + 3 * self.lag if self.steps else 0
        return [functools.partial(turn, index) for index in range(count)]

    def end(self):
        for number in range(len(self.pieces)):
            for phase in range(4):
                for copy in self.copies(number, phase):
                    copy.wait_send()


class Gather(Flow):
    def __init__(self, kinds, shards, sizes, ahead, lag):
        super().__init__(kinds, shards, sizes, ahead, lag)
        lead = tuple(sizes[axis] for axis in AXES)
        self.out_shape = [jax.ShapeDtypeStruct(lead + one.shape, one.dtype) for one in shards]
        self.out_specs = [HBM] * len(shards)
        self.scratch = self.semaphores

    def own_copy(self, number):
        array, window = self.pieces[number][0], self.window(number)
        return pltpu.make_async_copy(
            self.ins[array].at[window],
            self.outs[array].at[region(self.place, (), window)],
            self.own_sem.at[number],
        )

    def copies(self, number, phase):
        array, order, window = self.pieces[number][0], self.pieces[number][-1], self.window(number)
        axis = (order + ("c",))[phase]
        part = self.outs[array].at[region(self.place, order[:phase], window)]
        source = self.ins[array].at[window] if phase == 0 else part
        return [
            self.remote(number, axis, step, source, part) for step in range(1, self.sizes[axis])
        ]

    def take(self, number, phase):
        pass


class Scatter(Flow):
    def __init__(self, kinds, grads, sizes, ahead, lag):
        grads = [
            grad.reshape(tuple(sizes[axis] for axis in AXES) + (-1, grad.shape[-1]))
            for grad in grads
        ]
        super().__init__(kinds, grads, sizes, ahead, lag)
        self.out_shape = [jax.ShapeDtypeStruct(grad.shape[-2:], jnp.float32) for grad in grads]
        self.out_specs = [VMEM] * len(grads)
        self.scratch = []
        for _, _, rows, _, columns, order in self.pieces:

            def shape_of(full, rows=rows, columns=columns):
                return tuple(sizes[axis] for axis in AXES if axis in full) + (rows, columns)

            self.scratch += [pltpu.VMEM(shape_of(order), jnp.bfloat16)] * 2
            for phase in range(3):
                senders = sizes[order[2 - phase]] - 1
                self.scratch.append(
                    pltpu.VMEM((senders,) + shape_of(order[: 2 - phase]), jnp.bfloat16)
                )
        self.scratch += self.semaphores

    def own_copy(self, number):
        array = self.pieces[number][0]
        return pltpu.make_async_copy(
            self.ins[array].at[region(self.place, AXES[:3], self.window(number))],
            self.buffers[5 * number],
            self.own_sem.at[number],
        )

    def copies(self, number, phase):
        array, order = self.pieces[number][0], self.pieces[number][-1]
        axis = "c" if phase == 0 else order[3 - phase]
        found = []
        for step in range(1, self.sizes[axis]):
            peer = peer_at(self.place, axis, step, self.sizes)
            if phase == 0:
                source = self.ins[array].at[region(peer, AXES[:3], self.window(number))]
                target = self.buffers[5 * number + 1]
            else:
                full = order[: 3 - phase]
                where = tuple(slice(None) if one in full else peer[one] for one in AXES[:3])
                source = self.buffers[5 * number].at[where]
                target = self.buffers[5 * number + 1 + phase].at[step - 1]
            found.append(self.remote(number, axis, step, source, target))
        return found

    def take(self, number, phase):
        array, order = self.pieces[number][0], self.pieces[number][-1]
        total = self.buffers[5 * number]
        got = self.buffers[5 * number + 1 + phase]
        if phase == 0:
            total[...] = total[...] + got[...]
            return
        full = order[: 3 - phase]
        where = tuple(slice(None) if axis in full else self.place[axis] for axis in AXES[:3])
        value = total[where]
        senders = self.sizes[order[3 - phase]] - 1
        if phase == 3:
            value = value.astype(jnp.float32)
            for sender in range(senders):
                value = value + got[sender].astype(jnp.float32)
            self.outs[array][self.window(number)] = value
        else:
            for sender in range(senders):
                value = value + got[sender]
            total[where] = value


def run_flow(flow, collective_id, name):
    count = len(flow.operands)

    def kernel(*refs):
        flow.bind(refs[:count], refs[count : 2 * count], refs[2 * count :])
        greet_axes(flow.place, flow.sizes)
        flow.begin()
        for turn in flow.turns():
            turn()
        flow.end()

    return pl.pallas_call(
        kernel,
        out_shape=flow.out_shape,
        in_specs=[HBM] * count,
        out_specs=flow.out_specs,
        scratch_shapes=flow.scratch,
        compiler_params=pltpu.CompilerParams(
            collective_id=collective_id, has_side_effects=True, vmem_limit_bytes=40 << 20
        ),
        cost_estimate=cost_of(30),
        name=name,
    )(*flow.operands)


def unit_place(unit, sizes):
    chips = sizes["x"] * sizes["y"]
    inside = quotient(unit, sizes["z"], chips * sizes["c"])
    row = quotient(inside, sizes["x"], sizes["y"] * sizes["c"])
    core = quotient(inside, chips, sizes["c"])
    x = inside - row * sizes["x"]
    y = wrapped(row - core * sizes["y"] + x, sizes["y"])
    return {"x": x, "z": unit - inside * sizes["z"], "y": y, "c": core}


def own_unit(sizes):
    place = own_place(sizes)
    turned = lax.rem(place["y"] + sizes["y"] * sizes["x"] - place["x"], sizes["y"])
    inside = (place["c"] * sizes["y"] + turned) * sizes["x"] + place["x"]
    return inside * sizes["z"] + place["z"]


class Exchange:
    def __init__(self, sizes, batches, sequences):
        self.sizes = sizes
        self.batches = batches
        self.sequences = sequences
        self.heads = sizes["x"]
        self.devices = math.prod(sizes.values())
        self.units = batches * sequences * HEADS
        self.blocks = self.devices // sequences
        self.held = batches * HEADS
        assert self.units <= self.devices

    def my_block(self):
        return lax.axis_index("seq") * self.heads + lax.axis_index("head")

    def unit_for(self, slot, block):
        batch = quotient(slot, HEADS, self.batches)
        sequence = quotient(block, self.blocks, self.sequences)
        return (batch * self.sequences + sequence) * HEADS + slot - batch * HEADS

    def block_device(self, block):
        return {"head": lax.rem(block, self.heads), "seq": lax.div(block, self.heads)}

    def token_device(self, unit, slot):
        if self.sequences > 1:
            slot = slot + lax.rem(lax.div(unit, HEADS), self.sequences) * self.blocks
        return self.block_device(slot)

    def unit_device(self, slot, block):
        return device_of(unit_place(self.unit_for(slot, block), self.sizes), self.sizes)

    def slot_of(self, unit):
        batch = lax.div(unit, HEADS * self.sequences)
        return lax.min(batch * HEADS + lax.rem(unit, HEADS), self.held - 1)

    def is_me(self, device):
        return jnp.logical_and(
            device["head"] == lax.axis_index("head"), device["seq"] == lax.axis_index("seq")
        )

    def greet_all(self):
        barrier = pltpu.get_barrier_semaphore()

        def greet(step, carry):
            device = self.block_device(lax.rem(self.my_block() + step, self.devices))
            pl.semaphore_signal(barrier, inc=1, device_id=device, device_id_type=MESH)
            return carry

        lax.fori_loop(1, self.devices, greet, 0)
        pl.semaphore_wait(barrier, self.devices - 1)

    def send(self, source, target, send_sem, recv_sem, own_sem, device, wait):
        same = self.is_me(device)
        remote = pltpu.make_async_remote_copy(
            src_ref=source,
            dst_ref=target,
            send_sem=send_sem,
            recv_sem=recv_sem,
            device_id=device,
            device_id_type=MESH,
        )
        if not wait:
            pl.when(same)(pltpu.make_async_copy(source, target, own_sem).start)

        @pl.when(jnp.logical_not(same))
        def _():
            remote.wait_send() if wait else remote.start()

    def receive(self, target, recv_sem, own_sem, device):
        same = self.is_me(device)

        @pl.when(same)
        def _():
            pltpu.make_async_copy(target, target, own_sem).wait()

        @pl.when(jnp.logical_not(same))
        def _():
            pltpu.make_async_copy(target, target, recv_sem).wait()

    def to_units(self, source_at, target_at, send_sem, recv_sem, own_sem, wait, part=0, parts=1):
        block = self.my_block()
        spot = block - quotient(block, self.blocks, self.sequences) * self.blocks
        turned = lax.rem(block, self.held)

        def one(index, carry):
            slot = wrapped(index + turned, self.held)
            self.send(
                source_at(slot),
                target_at(spot),
                send_sem.at[index],
                recv_sem.at[spot],
                own_sem,
                self.unit_device(slot, block),
                wait,
            )
            return carry

        lax.fori_loop(part * self.held // parts, (part + 1) * self.held // parts, one, 0)

    def at_unit(self, target_at, recv_sem, own_sem):
        unit = own_unit(self.sizes)

        def one(spot, carry):
            self.receive(
                target_at(spot), recv_sem.at[spot], own_sem, self.token_device(unit, spot)
            )
            return carry

        lax.fori_loop(0, self.blocks, one, 0)

    def to_token(self, spot, source_at, target_at, send_sem, recv_sem, own_sem, wait):
        unit = own_unit(self.sizes)
        slot = self.slot_of(unit)
        self.send(
            source_at(spot),
            target_at(slot),
            send_sem.at[spot],
            recv_sem.at[slot],
            own_sem,
            self.token_device(unit, spot),
            wait,
        )

    def at_tokens(self, target_at, recv_sem, own_sem):
        block = self.my_block()

        def one(slot, carry):
            self.receive(
                target_at(slot), recv_sem.at[slot], own_sem, self.unit_device(slot, block)
            )
            return carry

        lax.fori_loop(0, self.held, one, 0)


PART = 128
PER = TILE // PART
GUARD = WINDOW // TILE
REACH = 2 * GUARD + 1
DOC_ROWS = 64
FAR = -1e30
FORWARD_AHEAD, FORWARD_FIRST, FORWARD_LAG = 3, 5, 2
BACKWARD_AHEAD, BACKWARD_FIRST, BACKWARD_LAG = 4, 4, 2


def unit_context(lengths, exchange, tokens):
    unit = own_unit(exchange.sizes)
    row = lax.min(lax.div(unit, HEADS), exchange.batches * exchange.sequences - 1)
    head = lax.rem(unit, HEADS)
    own = lax.dynamic_index_in_dim(lengths.reshape(-1, lengths.shape[-1]), row, 0, keepdims=False)
    ends = jnp.cumsum(own)
    place = jnp.arange(tokens, dtype=jnp.int32)
    document = jnp.sum((place[None, :] >= ends[:, None]).astype(jnp.int32), axis=0)
    inside = jnp.arange(DOC_ROWS, dtype=jnp.int32)[:, None] == document[None, :]
    real = jnp.arange(DOC_ROWS, dtype=jnp.int32)[:, None] < lengths.shape[-1]
    of_query = jnp.where(inside, FAR, 0.0)
    of_key = jnp.where(real & ~inside, 1.0, 0.0)
    blocks = tokens // PART
    shape = (DOC_ROWS, blocks, PART)
    slope = jnp.exp2(-8.0 * (head + 1).astype(jnp.float32) / HEADS)
    return (
        (slope * LOG2E).reshape(1),
        of_query.reshape(shape).transpose(1, 0, 2).astype(jnp.bfloat16),
        of_key.reshape(shape).transpose(1, 0, 2).astype(jnp.bfloat16),
    )


def side_by_side(ref, tile, rows):
    return jnp.concatenate([ref[tile * PER + part, rows, :] for part in range(PER)], axis=1)


ROW_Q, ROW_K, ROW_V = slice(0, 64), slice(64, 128), slice(128, 192)


def rows_at(tile):
    return pl.ds(pl.multiple_of(tile * TILE, TILE), TILE)


def part_at(block):
    return pl.ds(pl.multiple_of(block * PART, PART), PART)


def fill_biases(slope_ref, bias_ref):
    key = lax.broadcasted_iota(jnp.int32, (TILE, TILE), 0)
    query = lax.broadcasted_iota(jnp.int32, (TILE, TILE), 1)

    def one(step, carry):
        distance = jnp.abs(key - query + (step - GUARD) * TILE)
        bias = distance.astype(jnp.float32) * -slope_ref[0]
        bias_ref[step] = jnp.where(distance < WINDOW, bias, FAR)
        return carry

    lax.fori_loop(0, REACH, one, 0)


def fill_guards(unit_ref, key_ref, blocks):
    rows = GUARD * TILE
    feature = lax.broadcasted_iota(jnp.int32, (rows, PART), 1)
    away = jnp.where((feature >= 64) & (feature < 72), 1.0, 0.0).astype(jnp.bfloat16)
    for first in (0, rows + blocks * PART):
        key_ref[pl.ds(first, rows), :] = away
    for first in (0, GUARD * PER + blocks):
        unit_ref[pl.ds(first, GUARD * PER)] = jnp.zeros(
            (GUARD * PER,) + unit_ref.shape[1:], unit_ref.dtype
        )


def fill_keys(unit_ref, doc_ref, key_ref, blocks):
    def one(block, carry):
        there = block + GUARD * PER
        features = jnp.concatenate([unit_ref[there, ROW_K, :], doc_ref[block]], axis=0)
        key_ref[part_at(there), :] = features.T
        return carry

    lax.fori_loop(0, blocks, one, 0, unroll=4)


class Service:
    def __init__(self, flow, first, tiles):
        self.turns = flow.turns()
        self.first = first
        self.after = {}
        left = max(len(self.turns) - first, 0)
        for index in range(left):
            self.after.setdefault(index * tiles // left, []).append(self.turns[first + index])

    def begin(self, done=0):
        for turn in self.turns[done : self.first]:
            turn()

    def at(self, tile):
        for index, turns in self.after.items():

            @pl.when(tile == index)
            def _(turns=turns):
                for turn in turns:
                    turn()


def attention_forward(packed, exchange, context, collective_id, flow, first):
    blocks, held = exchange.blocks, exchange.held
    tiles = blocks // PER
    edge = GUARD * PER

    count = len(flow.operands)

    def kernel(slope_ref, query_doc_ref, key_doc_ref, packed_ref, *refs):
        out_ref, keep_ref, wide_ref, sum_ref = refs[count : count + 4]
        flow.bind(refs[:count], refs[count + 4 : 2 * count + 4], refs[2 * count + 14 :])
        (
            unit_ref,
            key_ref,
            bias_ref,
            score_ref,
            result_ref,
            to_sem,
            at_sem,
            back_sem,
            home_sem,
            own_sem,
        ) = refs[2 * count + 4 : 2 * count + 14]
        service = Service(flow, first, tiles)
        has_unit = own_unit(exchange.sizes) < exchange.units
        exchange.greet_all()

        def units(wait, part=0, parts=1):
            exchange.to_units(
                lambda slot: packed_ref.at[slot],
                lambda spot: unit_ref.at[edge + spot],
                to_sem,
                at_sem,
                own_sem.at[0],
                wait,
                part,
                parts,
            )

        def tokens(spot, wait):
            exchange.to_token(
                spot,
                lambda spot: result_ref.at[spot],
                lambda slot: out_ref.at[slot],
                back_sem,
                home_sem,
                own_sem.at[1],
                wait,
            )

        keep = pltpu.make_async_copy(unit_ref.at[pl.ds(edge, blocks)], keep_ref, own_sem.at[2])
        flow.begin()
        parts = 3 if first > 2 else 1
        units(False, 0, parts)

        @pl.when(has_unit)
        def _():
            fill_biases(slope_ref, bias_ref)
            fill_guards(unit_ref, key_ref, blocks)

        for part in range(1, parts):
            service.turns[part - 1]()
            units(False, part, parts)
        service.begin(parts - 1)

        @pl.when(has_unit)
        def _():
            exchange.at_unit(lambda spot: unit_ref.at[edge + spot], at_sem, own_sem.at[0])
            keep.start()
            fill_keys(unit_ref, key_doc_ref, key_ref, blocks)

        def one_tile(tile, carry):
            @pl.when(has_unit)
            def _():
                q_t = jnp.concatenate(
                    [
                        side_by_side(unit_ref, tile + GUARD, ROW_Q),
                        side_by_side(query_doc_ref, tile, slice(0, DOC_ROWS)),
                    ],
                    axis=0,
                )
                top = jnp.full((1, TILE), FAR, jnp.float32)
                for step in range(REACH):
                    raw = jnp.dot(
                        key_ref[rows_at(tile + step), :], q_t, preferred_element_type=jnp.float32
                    )
                    score = raw * (HEAD_DIM ** (-0.5) * LOG2E) + bias_ref[step]
                    score_ref[step] = score
                    top = jnp.maximum(top, jnp.max(score, axis=0, keepdims=True))
                total = jnp.zeros((1, TILE), jnp.float32)
                attended = jnp.zeros((HEAD_DIM, TILE), jnp.float32)
                for step in range(REACH):
                    probs = jnp.exp2(score_ref[step] - top)
                    total = total + jnp.sum(probs, axis=0, keepdims=True)
                    attended = attended + jnp.dot(
                        side_by_side(unit_ref, tile + step, ROW_V),
                        probs.astype(jnp.bfloat16),
                        preferred_element_type=jnp.float32,
                    )
                result = attended / total
                sum_ref[tile] = top + jnp.log2(total)
                for part in range(PER):
                    piece = result[:, part * PART : (part + 1) * PART]
                    wide_ref[tile * PER + part] = piece
                    result_ref[tile * PER + part] = piece.astype(jnp.bfloat16)
                    tokens(tile * PER + part, False)

            service.at(tile)
            return carry

        lax.fori_loop(0, tiles, one_tile, 0)
        units(True)

        exchange.at_tokens(lambda slot: out_ref.at[slot], home_sem, own_sem.at[1])

        @pl.when(has_unit)
        def _():
            def sent(spot, carry):
                tokens(spot, True)
                return carry

            lax.fori_loop(0, blocks, sent, 0)
            keep.wait()

        flow.end()

    return pl.pallas_call(
        kernel,
        out_shape=[
            jax.ShapeDtypeStruct((held, HEAD_DIM, PART), jnp.bfloat16),
            jax.ShapeDtypeStruct((blocks, 3 * HEAD_DIM, PART), jnp.bfloat16),
            jax.ShapeDtypeStruct((blocks, HEAD_DIM, PART), jnp.float32),
            jax.ShapeDtypeStruct((tiles, 1, TILE), jnp.float32),
        ]
        + flow.out_shape,
        in_specs=[SMEM, VMEM, VMEM, HBM] + [HBM] * count,
        out_specs=[HBM, HBM, VMEM, VMEM] + flow.out_specs,
        scratch_shapes=[
            pltpu.VMEM((blocks + 2 * edge, 3 * HEAD_DIM, PART), jnp.bfloat16),
            pltpu.VMEM(((blocks + 2 * edge) * PART, PART), jnp.bfloat16),
            pltpu.VMEM((REACH, TILE, TILE), jnp.float32),
            pltpu.VMEM((REACH, TILE, TILE), jnp.float32),
            pltpu.VMEM((blocks, HEAD_DIM, PART), jnp.bfloat16),
            pltpu.SemaphoreType.DMA((held,)),
            pltpu.SemaphoreType.DMA((blocks,)),
            pltpu.SemaphoreType.DMA((blocks,)),
            pltpu.SemaphoreType.DMA((held,)),
            pltpu.SemaphoreType.DMA((3,)),
        ]
        + flow.scratch,
        compiler_params=pltpu.CompilerParams(
            collective_id=collective_id, has_side_effects=True, vmem_limit_bytes=48 << 20
        ),
        cost_estimate=cost_of(60),
        name="attention_forward",
    )(*context, packed, *flow.operands)


def attention_backward(grad, unit_kept, exchange, context, collective_id, flow, first):
    blocks, held = exchange.blocks, exchange.held
    tiles = blocks // PER
    edge = GUARD * PER

    count = len(flow.operands)

    def kernel(
        slope_ref, query_doc_ref, key_doc_ref, wide_ref, sum_ref, grad_ref, kept_ref, *refs
    ):
        out_ref = refs[count]
        flow.bind(refs[:count], refs[count + 1 : 2 * count + 1], refs[2 * count + 13 :])
        (
            unit_ref,
            got_ref,
            key_ref,
            value_ref,
            bias_ref,
            total_ref,
            result_ref,
            to_sem,
            at_sem,
            back_sem,
            home_sem,
            own_sem,
        ) = refs[2 * count + 1 : 2 * count + 13]
        service = Service(flow, first, tiles)
        has_unit = own_unit(exchange.sizes) < exchange.units
        exchange.greet_all()

        def units(wait):
            exchange.to_units(
                lambda slot: grad_ref.at[slot],
                lambda spot: got_ref.at[spot],
                to_sem,
                at_sem,
                own_sem.at[0],
                wait,
            )

        def tokens(spot, wait):
            exchange.to_token(
                spot,
                lambda spot: result_ref.at[spot],
                lambda slot: out_ref.at[slot],
                back_sem,
                home_sem,
                own_sem.at[1],
                wait,
            )

        load = pltpu.make_async_copy(kept_ref, unit_ref.at[pl.ds(edge, blocks)], own_sem.at[2])
        flow.begin()
        units(False)

        @pl.when(has_unit)
        def _():
            load.start()
            fill_biases(slope_ref, bias_ref)
            fill_guards(unit_ref, key_ref, blocks)
            for first in (0, (edge + blocks) * PART):
                value_ref[pl.ds(first, edge * PART), :] = jnp.zeros(
                    (edge * PART, PART), value_ref.dtype
                )
            total_ref[...] = jnp.zeros_like(total_ref)
            load.wait()
            fill_keys(unit_ref, key_doc_ref, key_ref, blocks)

            def one(block, carry):
                there = block + edge
                value_ref[part_at(there), :] = unit_ref[there, 64:192, :].T
                return carry

            lax.fori_loop(0, blocks, one, 0, unroll=4)

        service.begin()

        @pl.when(has_unit)
        def _():
            exchange.at_unit(lambda spot: got_ref.at[spot], at_sem, own_sem.at[0])

        def finish(tile):
            for part in range(PER):
                block = tile * PER + part
                result_ref[block, 64:192, :] = total_ref[part_at(block + edge), :].T.astype(
                    jnp.bfloat16
                )
                tokens(block, False)

        def one_tile(tile, carry):
            @pl.when(has_unit)
            def _():
                q_part = side_by_side(unit_ref, tile + GUARD, ROW_Q)
                g_part = side_by_side(got_ref, tile, slice(0, 64))
                q_t = jnp.concatenate(
                    [q_part, side_by_side(query_doc_ref, tile, slice(0, DOC_ROWS))], axis=0
                )
                g_small = g_part * jnp.asarray(HEAD_DIM ** (-0.5), jnp.bfloat16)
                g_t = jnp.concatenate([jnp.zeros_like(g_small), g_small], axis=0)
                turned = jnp.concatenate([q_part, g_part], axis=0).T
                lane = lax.broadcasted_iota(jnp.int32, turned.shape, 1)
                none = jnp.zeros_like(turned)
                q_and_g = jnp.concatenate(
                    [jnp.where(lane < 64, turned, none), jnp.where(lane < 64, none, turned)],
                    axis=0,
                )
                wide_t = side_by_side(wide_ref, tile, slice(0, 64))
                mean = jnp.sum(g_small.astype(jnp.float32) * wide_t, axis=0, keepdims=True)
                sum_now = sum_ref[tile]
                grad_q = jnp.zeros((HEAD_DIM, TILE), jnp.float32)
                for step in range(REACH):
                    there = rows_at(tile + step)
                    raw = jnp.dot(key_ref[there, :], q_t, preferred_element_type=jnp.float32)
                    grad_probs = jnp.dot(
                        value_ref[there, :], g_t, preferred_element_type=jnp.float32
                    )
                    score = raw * (HEAD_DIM ** (-0.5) * LOG2E) + bias_ref[step]
                    probs = jnp.exp2(score - sum_now)
                    grad_raw = (probs * (grad_probs - mean)).astype(jnp.bfloat16)
                    total_ref[there, :] += jnp.dot(
                        jnp.concatenate([grad_raw, probs.astype(jnp.bfloat16)], axis=1),
                        q_and_g,
                        preferred_element_type=jnp.float32,
                    )
                    grad_q = grad_q + jnp.dot(
                        side_by_side(unit_ref, tile + step, ROW_K),
                        grad_raw,
                        preferred_element_type=jnp.float32,
                    )
                for part in range(PER):
                    result_ref[tile * PER + part, ROW_Q, :] = grad_q[
                        :, part * PART : (part + 1) * PART
                    ].astype(jnp.bfloat16)

                @pl.when(tile >= GUARD)
                def _():
                    finish(tile - GUARD)

            service.at(tile)
            return carry

        lax.fori_loop(0, tiles, one_tile, 0)
        units(True)

        @pl.when(has_unit)
        def _():
            def rest(tile, carry):
                finish(tile)
                return carry

            lax.fori_loop(max(tiles - GUARD, 0), tiles, rest, 0)

        exchange.at_tokens(lambda slot: out_ref.at[slot], home_sem, own_sem.at[1])

        @pl.when(has_unit)
        def _():
            def sent(spot, carry):
                tokens(spot, True)
                return carry

            lax.fori_loop(0, blocks, sent, 0)

        flow.end()

    return pl.pallas_call(
        kernel,
        out_shape=[jax.ShapeDtypeStruct((held, 3 * HEAD_DIM, PART), jnp.bfloat16)] + flow.out_shape,
        in_specs=[SMEM, VMEM, VMEM, VMEM, VMEM, HBM, HBM] + [HBM] * count,
        out_specs=[HBM] + flow.out_specs,
        scratch_shapes=[
            pltpu.VMEM((blocks + 2 * edge, 3 * HEAD_DIM, PART), jnp.bfloat16),
            pltpu.VMEM((blocks, HEAD_DIM, PART), jnp.bfloat16),
            pltpu.VMEM(((blocks + 2 * edge) * PART, PART), jnp.bfloat16),
            pltpu.VMEM(((blocks + 2 * edge) * PART, PART), jnp.bfloat16),
            pltpu.VMEM((REACH, TILE, TILE), jnp.float32),
            pltpu.VMEM(((blocks + 2 * edge) * PART, PART), jnp.float32),
            pltpu.VMEM((blocks, 3 * HEAD_DIM, PART), jnp.bfloat16),
            pltpu.SemaphoreType.DMA((held,)),
            pltpu.SemaphoreType.DMA((blocks,)),
            pltpu.SemaphoreType.DMA((blocks,)),
            pltpu.SemaphoreType.DMA((held,)),
            pltpu.SemaphoreType.DMA((3,)),
        ]
        + flow.scratch,
        compiler_params=pltpu.CompilerParams(
            collective_id=collective_id, has_side_effects=True, vmem_limit_bytes=60 << 20
        ),
        cost_estimate=cost_of(70),
        name="attention_backward",
    )(*context, *unit_kept[1:], grad, unit_kept[0], *flow.operands)


def layer_norm(summed, gain, shift):
    centre = jnp.mean(summed, axis=-1, keepdims=True)
    centred = summed - centre
    variance = jnp.mean(centred * centred, axis=-1, keepdims=True)
    return centred * lax.rsqrt(variance + 1e-12) * gain + shift


def geglu(gate, upper):
    return jax.nn.gelu(gate, approximate=False) * upper


def dot(a, b, a_axis, b_axis):
    return lax.dot_general(
        a, b, (((a_axis,), (b_axis,)), ((), ())), preferred_element_type=jnp.float32
    )


def layer_forward(hidden, qkv_w, others, kinds, shards, exchange, context, collective_id):
    batches = exchange.batches
    tokens = hidden.shape[0] // batches
    hidden_low = lax.optimization_barrier(hidden.astype(jnp.bfloat16))
    packed = dot(qkv_w, hidden_low, 0, 1).astype(jnp.bfloat16)
    packed = packed.reshape(3, HEADS, HEAD_DIM, batches, tokens)
    packed = packed.transpose(3, 1, 0, 2, 4).reshape(batches * HEADS, 3 * HEAD_DIM, tokens)
    attended, unit_packed, wide, sums, *gathered = attention_forward(
        packed,
        exchange,
        context,
        collective_id,
        Gather(kinds, shards, exchange.sizes, FORWARD_AHEAD, FORWARD_LAG),
        FORWARD_FIRST if kinds else 0,
    )
    out_w, up_w, down_w = others + [one.reshape(-1, one.shape[-1]) for one in gathered]
    norm_f = out_w[:, D : D + 4].astype(jnp.float32)
    out_w = out_w[:, :D]
    attn_t = attended.reshape(batches, D, tokens)
    attn_low = attn_t.transpose(0, 2, 1).reshape(batches * tokens, D)
    mixed = hidden + dot(attn_low, out_w, 1, 0)
    normed = layer_norm(mixed, norm_f[:, 0], norm_f[:, 1])
    normed_low = normed.astype(jnp.bfloat16)
    upper = dot(normed_low, up_w, 1, 0)
    act_low = geglu(upper[:, :FF], upper[:, FF:]).astype(jnp.bfloat16)
    second = normed + dot(act_low, down_w, 1, 0)
    result = layer_norm(second, norm_f[:, 2], norm_f[:, 3])
    weights = (qkv_w, out_w, up_w, down_w, norm_f)
    unit_kept = (unit_packed, wide, sums)
    kept = (hidden_low, unit_kept, attn_low, mixed, normed_low, upper, act_low, second)
    return result, weights, kept


def layer_backward(grad_result, weights, kept, exchange, context, collective_id):
    qkv_w, out_w, up_w, down_w, norm_f = weights
    hidden_low, unit_kept, attn_low, mixed, normed_low, upper, act_low, second = kept
    batches = exchange.batches
    tokens = grad_result.shape[0] // batches
    pull_two = jax.vjp(layer_norm, second, norm_f[:, 2], norm_f[:, 3])[1]
    grad_second, grad_gain_two, grad_shift_two = pull_two(grad_result)
    grad_branch = grad_second.astype(jnp.bfloat16)
    grad_act = dot(grad_branch, down_w, 1, 1)
    pull_gate = jax.vjp(geglu, upper[:, :FF], upper[:, FF:])[1]
    grad_gate, grad_upper = pull_gate(grad_act)
    grad_up_low = jnp.concatenate([grad_gate, grad_upper], axis=1).astype(jnp.bfloat16)
    grad_normed = grad_second + dot(grad_up_low, up_w, 1, 1)
    pull_one = jax.vjp(layer_norm, mixed, norm_f[:, 0], norm_f[:, 1])[1]
    grad_mixed, grad_gain_one, grad_shift_one = pull_one(grad_normed)
    grad_attn = grad_mixed.astype(jnp.bfloat16)
    grad_heads = dot(out_w, grad_attn, 1, 1).astype(jnp.bfloat16)
    grad_heads = grad_heads.reshape(HEADS, HEAD_DIM, batches, tokens)
    grad_heads = grad_heads.transpose(2, 0, 1, 3).reshape(batches * HEADS, HEAD_DIM, tokens)
    grad_norm = jnp.stack([grad_gain_one, grad_shift_one, grad_gain_two, grad_shift_two], axis=1)
    grad_out_w = jnp.concatenate(
        [
            dot(attn_low, grad_attn, 0, 0).astype(jnp.bfloat16),
            jnp.pad(grad_norm.astype(jnp.bfloat16), ((0, 0), (0, NORM_PAD - 4))),
        ],
        axis=1,
    )
    grad_up_w = dot(normed_low, grad_up_low, 0, 0).astype(jnp.bfloat16)
    grad_down_w = dot(act_low, grad_branch, 0, 0).astype(jnp.bfloat16)
    flow = Scatter(
        ["down", "up", "out"],
        [grad_down_w, grad_up_w, grad_out_w],
        exchange.sizes,
        BACKWARD_AHEAD,
        BACKWARD_LAG,
    )
    packed_grad, *totals = attention_backward(
        grad_heads,
        unit_kept,
        exchange,
        context,
        collective_id,
        flow,
        BACKWARD_FIRST,
    )
    packed_grad = packed_grad.reshape(batches, HEADS, 3, HEAD_DIM, tokens)
    packed_grad = packed_grad.transpose(0, 4, 2, 1, 3).reshape(batches * tokens, 3 * D)
    grad_hidden = grad_mixed + dot(packed_grad, qkv_w, 1, 1)
    grad_qkv_w = dot(hidden_low, packed_grad, 0, 0).astype(jnp.bfloat16)
    return grad_hidden, grad_qkv_w, totals


def adamw(weight, first, second, grad, rate):
    first_new = beta_one * first + (1.0 - beta_one) * grad
    second_new = beta_two * second + (1.0 - beta_two) * grad * grad
    first_hat = first_new / (1.0 - beta_one**STEP)
    second_hat = second_new / (1.0 - beta_two**STEP)
    weight_new = weight - rate * (first_hat / (jnp.sqrt(second_hat) + adam_eps) + decay * weight)
    return (first_new, second_new, weight_new)


def body(
    inputs,
    cotangent,
    lengths,
    qkv_weight,
    qkv_first,
    qkv_second,
    out_weight,
    out_first,
    out_second,
    up_weight,
    up_first,
    up_second,
    down_weight,
    down_first,
    down_second,
    norm_params,
    norm_first,
    norm_second,
):
    masters = (qkv_weight, out_weight, up_weight, down_weight, norm_params)
    states = (
        (qkv_first, qkv_second),
        (out_first, out_second),
        (up_first, up_second),
        (down_first, down_second),
        (norm_first, norm_second),
    )
    sizes = grid_sizes(lax.axis_size("seq"))
    batches, tokens = inputs.shape[:2]
    exchange = Exchange(sizes, batches, lengths.shape[1])
    context = unit_context(lengths, exchange, exchange.blocks * tokens)
    norm_wide = jnp.pad(norm_params, ((0, 0), (0, 0), (0, NORM_PAD - 4)))
    sources = (qkv_weight, jnp.concatenate([out_weight, norm_wide], axis=2), up_weight, down_weight)
    shards = [[source[layer].astype(jnp.bfloat16) for source in sources] for layer in range(LAYERS)]
    qkv_w = run_flow(Gather(["qkv"], shards[0][:1], sizes, 2, 1), 0, "gather_weights")[0]
    qkv_w = qkv_w.reshape(-1, qkv_w.shape[-1])
    everyone = ("head", "seq")
    later = [lax.all_gather(shard, everyone, axis=0, tiled=True) for shard in shards[1]]

    hidden = inputs.reshape(batches * tokens, D).astype(jnp.float32)
    weights_all, kept_all = [], []
    for layer in range(LAYERS):
        hidden, weights, kept = layer_forward(
            hidden,
            later[0] if layer else qkv_w,
            later[1:] if layer else [],
            [] if layer else ["out", "up", "down"],
            [] if layer else shards[0][1:],
            exchange,
            context,
            1 + layer,
        )
        weights_all.append(weights)
        kept_all.append(kept)
    outputs = hidden.reshape(batches, tokens, D)
    grad_hidden = cotangent.reshape(batches * tokens, D).astype(jnp.float32)
    totals = [[None] * 4 for _ in range(LAYERS)]
    late = []
    for layer in reversed(range(LAYERS)):
        grad_hidden, grad_qkv_w, done = layer_backward(
            grad_hidden,
            weights_all[layer],
            kept_all[layer],
            exchange,
            context,
            1 + LAYERS + layer,
        )
        totals[layer][3], totals[layer][2], totals[layer][1] = done
        late.append(grad_qkv_w)
    last = Scatter(["qkv"] * LAYERS, late, sizes, 4, 2)
    totals[1][0], totals[0][0] = run_flow(last, 1 + 2 * LAYERS, "scatter_grads")
    input_grad = grad_hidden.reshape(batches, tokens, D)

    results = [outputs, input_grad]
    kinds = [
        jnp.stack([totals[layer][0] for layer in range(LAYERS)]),
        jnp.stack([totals[layer][1][:, :D] for layer in range(LAYERS)]),
        jnp.stack([totals[layer][2] for layer in range(LAYERS)]),
        jnp.stack([totals[layer][3] for layer in range(LAYERS)]),
        jnp.stack([totals[layer][1][:, D : D + 4] for layer in range(LAYERS)]),
    ]
    new_weights = []
    for kind in range(5):
        first_new, second_new, weight_new = adamw(
            masters[kind], states[kind][0], states[kind][1], kinds[kind], learn_rates[kind]
        )
        results += [kinds[kind], first_new, second_new, weight_new]
        new_weights.append(weight_new)
    results += [member.astype(jnp.bfloat16) for member in new_weights[:4]]
    return tuple(results)


def solution(mesh):
    tokens = P(None, ("seq", "head"), None)
    rows = P(None, ("head", "seq"), None)
    in_specs = (tokens, tokens, P()) + (rows,) * 15
    out_specs = (tokens, tokens) + (rows,) * 24
    return jax.shard_map(body, mesh=mesh, in_specs=in_specs, out_specs=out_specs, check_vma=False)
```

time: 2160 us -> 762 us (0.35)
  waiting for transfers between devices: 842 us -> 0.09 us
  Pallas kernels: 0 us -> 581 us
  matrix products: 498 us -> 83.9 us
  starting transfers between devices: 245 us -> 0.16 us
  local copies, waits for them, and re-layouts: 273 us -> 43.5 us
  other arithmetic: 165 us -> 32.5 us
  blocking collectives: 101 us -> 0 us
    pallas_call x0 -> x6, Pallas kernels: none -> 581 us  [the longest x2 287 us: attention_backward(): pl.pallas_call(kernel, out_shape=[jax.ShapeDtypeStruct((held, 3 * HEAD_DI...]
    reduce_scatter x3 -> x0, waiting for transfers between devices: 561 us -> none  [the longest x1 351 us: body(): lax.psum_scatter(totals[2], ('head', 'seq'), scatter_dimension=1, tiled=T...]
    dot_general x72 -> x24, matrix products: 498 us -> 83.9 us  [dot(): lax.dot_general(a, b, (((a_axis,), (b_axis,)), ((), ())), preferred_eleme...]
    ppermute x64 -> x0, starting transfers between devices: 182 us -> none  [shifted(): lax.ppermute(value, axis, [(source, source + steps) for source in range(f...]
    all_gather x4, waiting for transfers between devices: 98.3 us -> 0.03 us  [body(): lax.all_gather(shard, everyone, axis=0, tiled=True)]
    unnamed x9 -> x4, waiting for transfers between devices: 96.2 us -> 0.07 us
    ppermute x64 -> x0, waiting for transfers between devices: 66.3 us -> none  [shifted(): lax.ppermute(value, axis, [(source, source + steps) for source in range(f...]
    all_to_all x16 -> x0, starting transfers between devices: 62.6 us -> none  [the longest x4 16.8 us: layer_forward(): lax.all_to_all(attn_heads, 'head', split_axis=0, concat_axis=1, tiled=True)]
  transfers between devices with their start and end apart: 88 -> 4, of which waited for: 16 -> 0; matrix products, arithmetic and copies ran while one was open for 38% -> 7% of each run, Pallas kernels for 0% -> 31%
where the time goes in v1:
time: 762 us; the launch traced here: 756 us
  Pallas kernels  581 us (76%)
  matrix products  83.9 us (11%)
  local copies, waits for them, and re-layouts  43.5 us (6%)
  other arithmetic  32.5 us (4%)
  between operations  15.5 us (2%)
    pallas_call x2, Pallas kernels, attention_backward(): pl.pallas_call(kernel, out_shape=[jax.ShapeDtypeStruct((held, 3 * HEAD_DI...  287 us
    pallas_call x2, Pallas kernels, attention_forward(): pl.pallas_call(kernel, out_shape=[jax.ShapeDtypeStruct((held, HEAD_DIM, P...  198 us
    pallas_call x2, Pallas kernels, run_flow(): pl.pallas_call(kernel, out_shape=flow.out_shape, in_specs=[HBM] * count,...  95.5 us
    dot_general x24, matrix products, dot(): lax.dot_general(a, b, (((a_axis,), (b_axis,)), ((), ())), preferred_eleme...  83.9 us
    unnamed x194, local copies, waits for them, and re-layouts  15.9 us
    convert_element_type x2, other arithmetic, layer_forward(): act_low = geglu(upper[:, :FF], upper[:, FF:]).astype(jnp.bfloat16)  15.4 us
  transfers between devices with their start and end apart: 4, of which 0 were waited for; matrix products, arithmetic and copies ran while one was open for 7% of the time, Pallas kernels for 31%

profile of v1, /device:TPU:0, one launch (start us, length us, event | category | flops | bytes accessed | tf_op | source)
XLA Modules:
  0.0 756.3 jit_solution(3352288901095184768)
XLA Ops:
  14.9 37.3 %gather_weights.1 = bf16[2,4,2,2,24,2304]{5,4,3,2,1,0:T(8,128)(2,1)S(1)} custom-call(bf16[24,2304]{1,0:T(8,128)(2,1)S(1)} %get-tuple-element.133.refs_0_), custom_call_target="tpu_custom_call" | custom-call | bytes 110700000 | tf_op jit(solution)/shard_map/gather_weights/pallas_call | solution.py:312
  56.1 132.9 %attention_forward.2 = (bf16[24,64,128]{2,1,0:T(8,128)(2,1)S(1)}, bf16[32,192,128]{2,1,0:T(8,128)(2,1)}, f32[32,64,128]{2,1,0:T(8,128)S(1)}, f32[16,1,256]{2,1,0...) custom-call(f32[1]{0:T(128)} %bitcast.1.slope_ref, ...), custom_call_target="tpu_custom_call" | custom-call | bytes 221400000 | tf_op jit(solution)/shard_map/attention_forward/pallas_call | solution.py:707
  195.4 5.5 fusion.90
  200.9 7.7 %multiply_convert_fusion.3 = (bf16[256,3072]{1,0:T(8,128)(2,1)S(1)}, f32[256,3072]{1,0:T(8,128)}) fusion(f32[256,6144]{1,0:T(8,128)S(1)} %fusion.90), kind=kLoop, calls=%fused_computation.43 | loop fusion | flops 51904512 | bytes 11010048 | tf_op jit(solution)/shard_map/convert_element_type | solution.py:972
  213.6 4.1 fusion.8
  220.1 3.5 reshape.362
  225.2 65.6 %attention_forward.3 = (bf16[24,64,128]{2,1,0:T(8,128)(2,1)S(1)}, bf16[32,192,128]{2,1,0:T(8,128)(2,1)S(1)}, f32[32,64,128]{2,1,0:T(8,128)S(1)}, f32[16,1,256]{2,1,0:T(1,128)S(1)}) custom-call(f32[1]{0:T(128)} %bitcast.1.slope_ref, bf16[32,64,128]{2,1,0:T(8,128)(2,1)S(1)} %get-tuple-element.137.query_doc_ref, ...), custom_call_target="tpu_custom_call" | custom-call | bytes 221400000 | tf_op jit(solution)/shard_map/attention_forward/pallas_call | solution.py:707
  297.3 5.3 fusion.2
  305.3 7.7 %multiply_convert_fusion.2 = (bf16[256,3072]{1,0:T(8,128)(2,1)S(1)}, f32[256,3072]{1,0:T(8,128)}) fusion(f32[256,6144]{1,0:T(8,128)S(1)} %fusion.2), kind=kLoop, calls=%fused_computation.30 | loop fusion | flops 51904512 | bytes 11010048 | tf_op jit(solution)/shard_map/convert_element_type | solution.py:972
  313.0 3.9 fusion.113
  319.4 3.7 convolution_convert_fusion.5
  323.1 5.0 add_convert_fusion.1
  328.2 5.6 convolution_convert_fusion.1
  333.9 2.9 multiply_reduce_fusion.4
  342.7 142.1 %attention_backward.2 = (bf16[24,192,128]{2,1,0:T(8,128)(2,1)}, f32[96,768]{1,0:T(8,128)}, f32[24,6144]{1,0:T(8,128)}, f32[24,896]{1,0:T(8,128)}) custom-call(f32[1]{0:T(128)} %bitcast.1.slope_ref, bf16[32,64,128]{2,1,0:T(8,128)(2,1)} %copy-done.4, bf16[32,64,128]{2,1,0:T(8,128)(2,1)} %copy-done.3, f32[32,64,128]{2,1,0:T(8,128)} %copy-done.9, ...), custom_call_target="tpu_custom_call" | custom-call | bytes 258300000 | tf_op jit(solution)/shard_map/attention_backward/pallas_call | solution.py:903
  487.3 3.5 multiply_reduce_fusion
  492.3 3.9 convolution_convert_fusion.4
  496.2 8.5 %add_convert_fusion = (bf16[256,3072]{1,0:T(8,128)(2,1)}, bf16[256,3072]{1,0:T(8,128)(2,1)}) fusion(f32[256,3072]{1,0:T(8,128)S(1)} %copy-done.22, f32[256,6144]{1,0:T(8,128)S(1)} %bitcast.159, bf16[3072,768]{1,0:T(8,128)(2,1)} %bitcast.198, f32[256,768]{1,0:T(8,128)S(1)} %get-tuple-element.114, f32[256]{0:T(256)S(1)} %negate_multiply_fusion.3), kind=kOutput, calls=%fused_computation.27 | convolution fusion | flops 1222508544 | bytes 18088960 | tf_op jit(solution)/shard_map/dot_general | solution.py:943
  504.8 8.4 %multiply_reduce_fusion.1 = (bf16[768]{0:T(1024)(128)(2,1)S(1)}, f32[256]{0:T(256)S(1)}, bf16[768]{0:T(1024)(128)(2,1)S(1)}, f32[256,768]{1,0:T(8,128)S(1)}) fusion(f32[256,768]{1,0:T(8,128)S(1)} %get-tuple-element.139, f32[256]{0:T(256)S(1)} %copy-done.61, f32[256]{0:T(256)S(1)} %copy-done.59, f32[768]{0:T(1024)S(1)} %get-tuple-element.86, ...), kind=kOutput, calls=%fused_computation.112 | convolution fusion | flops 2424174848 | bytes 14952448 | tf_op jit(solution)/shard_map/dot_general | solution.py:943
  513.3 5.7 convolution_convert_fusion
  520.8 2.9 convolution_convert_fusion.3
  526.4 144.7 %attention_backward.3 = (bf16[24,192,128]{2,1,0:T(8,128)(2,1)}, f32[96,768]{1,0:T(8,128)}, f32[24,6144]{1,0:T(8,128)}, f32[24,896]{1,0:T(8,128)}) custom-call(f32[1]{0:T(128)} %bitcast.1.slope_ref, bf16[32,64,128]{2,1,0:T(8,128)(2,1)} %copy-done.4, bf16[32,64,128]{2,1,0:T(8,128)(2,1)} %copy-done.3, f32[32,64,128]{2,1,0:T(8,128)} %copy-done.8, ...), custom_call_target="tpu_custom_call" | custom-call | bytes 258300000 | tf_op jit(solution)/shard_map/attention_backward/pallas_call | solution.py:903
  673.7 3.2 convolution_add_fusion.2
  682.9 58.2 %scatter_grads.1 = (f32[24,2304]{1,0:T(8,128)S(1)}, f32[24,2304]{1,0:T(8,128)S(1)}) custom-call(bf16[2,4,2,2,24,2304]{5,4,3,2,1,0:T(8,128)(2,1)S(1)} %bitcast.142, bf16[2,4,2,2,24,2304]{5,4,3,2,1,0:T(8,128)(2,1)S(1)} %bitcast.141), custom_call_target="tpu_custom_call" | custom-call | bytes 110700000 | tf_op jit(solution)/shard_map/scatter_grads/pallas_call | solution.py:312
  (301 shorter events, 68.9 us)
Async XLA Ops:
  7.2 204.2 %all-gather.11.cloned.1.call-start = ((), (), s32[]{:S(2)}) async-start(), calls=%async_computation.1 | async-start | bytes 1419264 | tf_op jit(solution)/shard_map/all_gather | solution.py:1080
  9.7 203.9 %all-gather.9.cloned.1.call-start = ((), (), s32[]{:S(2)}) async-start(), calls=%async_computation | async-start | bytes 3649536 | tf_op jit(solution)/shard_map/all_gather | solution.py:1080
  11.5 285.3 %all-gather.13.cloned.1.call-start = ((), (), s32[]{:S(2)}) async-start(), calls=%async_computation.2 | async-start | bytes 9732096 | tf_op jit(solution)/shard_map/all_gather | solution.py:1080
  13.6 299.4 %all-gather.15.cloned.1.call-start = ((), (), s32[]{:S(2)}) async-start(), calls=%async_computation.3 | async-start | bytes 4866048 | tf_op jit(solution)/shard_map/all_gather | solution.py:1080
  56.0 169.1 %copy-start.3 = (bf16[32,64,128]{2,1,0:T(8,128)(2,1)}, bf16[32,64,128]{2,1,0:T(8,128)(2,1)S(1)}, u32[]{:S(2)}) copy-start(bf16[32,64,128]{2,1,0:T(8,128)(2,1)S(1)} %get-tuple-element.136.key_doc_ref) | copy-start | bytes 1572868
  56.1 169.1 %copy-start.4 = (bf16[32,64,128]{2,1,0:T(8,128)(2,1)}, bf16[32,64,128]{2,1,0:T(8,128)(2,1)S(1)}, u32[]{:S(2)}) copy-start(bf16[32,64,128]{2,1,0:T(8,128)(2,1)S(1)} %get-tuple-element.137.query_doc_ref) | copy-start | bytes 1572868
  195.3 99.2 %copy-start.65 = (f32[768]{0:T(1024)}, f32[768]{0:T(1024)S(1)}, u32[]{:S(2)}) copy-start(f32[768]{0:T(1024)S(1)} %get-tuple-element.83) | copy-start | bytes 9220
  210.2 84.3 %copy-start.18 = (f32[256,768]{1,0:T(8,128)}, f32[256,768]{1,0:T(8,128)S(1)}, u32[]{:S(2)}) copy-start(f32[256,768]{1,0:T(8,128)S(1)} %get-tuple-element.141) | copy-start | bytes 2359300
  210.2 84.3 %copy-start.68 = (f32[256]{0:T(256)}, f32[256]{0:T(256)S(1)}, u32[]{:S(2)}) copy-start(f32[256]{0:T(256)S(1)} %broadcast_multiply_fusion.2) | copy-start | bytes 3076
  210.5 84.0 %copy-start.72 = (f32[256]{0:T(256)}, f32[256]{0:T(256)S(1)}, u32[]{:S(2)}) copy-start(f32[256]{0:T(256)S(1)} %fusion.79) | copy-start | bytes 3076
  342.7 144.6 %copy-start.19 = (f32[256,768]{1,0:T(8,128)S(1)}, f32[256,768]{1,0:T(8,128)}, u32[]{:S(2)}) copy-start(f32[256,768]{1,0:T(8,128)} %copy-done.18) | copy-start | bytes 2359300
  342.7 144.6 %copy-start.26 = (f32[256,768]{1,0:T(8,128)S(1)}, f32[256,768]{1,0:T(8,128)}, u32[]{:S(2)}) copy-start(f32[256,768]{1,0:T(8,128)} %copy-done.25) | copy-start | bytes 2359300
  342.7 144.6 %copy-start.66 = (f32[768]{0:T(1024)S(1)}, f32[768]{0:T(1024)}, u32[]{:S(2)}) copy-start(f32[768]{0:T(1024)} %copy-done.65) | copy-start | bytes 9220
  342.7 144.6 %copy-start.69 = (f32[256]{0:T(256)S(1)}, f32[256]{0:T(256)}, u32[]{:S(2)}) copy-start(f32[256]{0:T(256)} %copy-done.68) | copy-start | bytes 3076
  342.7 144.6 %copy-start.73 = (f32[256]{0:T(256)S(1)}, f32[256]{0:T(256)}, u32[]{:S(2)}) copy-start(f32[256]{0:T(256)} %copy-done.72) | copy-start | bytes 3076
  526.4 147.2 %copy-start.6 = (bf16[2,4,2,2,24,2304]{5,4,3,2,1,0:T(8,128)(2,1)S(1)}, bf16[2,4,2,2,24,2304]{5,4,3,2,1,0:T(8,128)(2,1)}, u32[]{:S(2)}) copy-start(bf16[2,4,2,2,24,2304]{5,4,3,2,1,0:T(8,128)(2,1)} %copy-done.5) | copy-start | bytes 10616836
  682.8 58.3 %copy-start.29 = (f32[2,24,2304]{2,1,0:T(8,128)S(1)}, f32[2,24,2304]{2,1,0:T(8,128)}, u32[]{:S(2)}) copy-start(f32[2,24,2304]{2,1,0:T(8,128)} %param.21) | copy-start | bytes 1327108
  682.8 58.3 %copy-start.46 = (f32[2,24,2304]{2,1,0:T(8,128)S(1)}, f32[2,24,2304]{2,1,0:T(8,128)}, u32[]{:S(2)}) copy-start(f32[2,24,2304]{2,1,0:T(8,128)} %param.23) | copy-start | bytes 1327108
  682.8 58.3 %copy-start.47 = (f32[2,24,2304]{2,1,0:T(8,128)S(1)}, f32[2,24,2304]{2,1,0:T(8,128)}, u32[]{:S(2)}) copy-start(f32[2,24,2304]{2,1,0:T(8,128)} %param.22) | copy-start | bytes 1327108
  682.8 59.8 %copy-start.43 = (f32[2,24,768]{2,1,0:T(8,128)S(1)}, f32[2,24,768]{2,1,0:T(8,128)}, u32[]{:S(2)}) copy-start(f32[2,24,768]{2,1,0:T(8,128)} %param.24) | copy-start | bytes 442372
  682.8 59.7 %copy-start.52 = (f32[1,24,768]{2,1,0:T(8,128)S(1)}, f32[1,24,768]{2,1,0:T(8,128)}, u32[]{:S(2)}) copy-start(f32[1,24,768]{2,1,0:T(8,128)} %get-tuple-element.149) | copy-start | bytes 221188
  682.8 59.7 %copy-start.53 = (f32[1,24,768]{2,1,0:T(8,128)S(1)}, f32[1,24,768]{2,1,0:T(8,128)}, u32[]{:S(2)}) copy-start(f32[1,24,768]{2,1,0:T(8,128)} %get-tuple-element.150) | copy-start | bytes 221188
  682.9 59.7 %copy-start.54 = (f32[2,24,768]{2,1,0:T(8,128)S(1)}, f32[2,24,768]{2,1,0:T(8,128)}, u32[]{:S(2)}) copy-start(f32[2,24,768]{2,1,0:T(8,128)} %param.26) | copy-start | bytes 442372
  682.9 59.7 %copy-start.55 = (f32[2,24,768]{2,1,0:T(8,128)S(1)}, f32[2,24,768]{2,1,0:T(8,128)}, u32[]{:S(2)}) copy-start(f32[2,24,768]{2,1,0:T(8,128)} %param.25) | copy-start | bytes 442372
  (76 other events, 396.9 us)
Sparse Core Ops, SparseCore 0:
  11.5 60.4 all-gather.10
  75.4 75.9 all-gather.8
  154.9 83.0 all-gather.12
  241.4 70.7 all-gather.14

commit v2 on v1

--- a/solution.py
+++ b/solution.py
@@ -935,8 +935,18 @@
     return centred * lax.rsqrt(variance + 1e-12) * gain + shift
 
 
+def normal_share(gate):
+    return 0.5 * lax.erf(gate * math.sqrt(0.5)) + 0.5
+
+
 def geglu(gate, upper):
-    return jax.nn.gelu(gate, approximate=False) * upper
+    return gate * normal_share(gate) * upper
+
+
+def geglu_backward(gate, upper, grad):
+    share = normal_share(gate)
+    slope = share + gate * jnp.exp(-0.5 * gate * gate) * (1.0 / math.sqrt(2.0 * math.pi))
+    return grad * upper * slope, grad * (gate * share)
 
 
 def dot(a, b, a_axis, b_axis):
@@ -958,9 +968,10 @@
         context,
         collective_id,
         Gather(kinds, shards, exchange.sizes, FORWARD_AHEAD, FORWARD_LAG),
-        FORWARD_FIRST if kinds else 0,
+        FORWARD_FIRST if len(kinds) > 1 else 1,
     )
-    out_w, up_w, down_w = others + [one.reshape(-1, one.shape[-1]) for one in gathered]
+    gathered = [one.reshape(-1, one.shape[-1]) for one in gathered]
+    out_w, up_w, down_w = gathered + others
     norm_f = out_w[:, D : D + 4].astype(jnp.float32)
     out_w = out_w[:, :D]
     attn_t = attended.reshape(batches, D, tokens)
@@ -987,8 +998,7 @@
     grad_second, grad_gain_two, grad_shift_two = pull_two(grad_result)
     grad_branch = grad_second.astype(jnp.bfloat16)
     grad_act = dot(grad_branch, down_w, 1, 1)
-    pull_gate = jax.vjp(geglu, upper[:, :FF], upper[:, FF:])[1]
-    grad_gate, grad_upper = pull_gate(grad_act)
+    grad_gate, grad_upper = geglu_backward(upper[:, :FF], upper[:, FF:], grad_act)
     grad_up_low = jnp.concatenate([grad_gate, grad_upper], axis=1).astype(jnp.bfloat16)
     grad_normed = grad_second + dot(grad_up_low, up_w, 1, 1)
     pull_one = jax.vjp(layer_norm, mixed, norm_f[:, 0], norm_f[:, 1])[1]
@@ -1077,7 +1087,8 @@
     qkv_w = run_flow(Gather(["qkv"], shards[0][:1], sizes, 2, 1), 0, "gather_weights")[0]
     qkv_w = qkv_w.reshape(-1, qkv_w.shape[-1])
     everyone = ("head", "seq")
-    later = [lax.all_gather(shard, everyone, axis=0, tiled=True) for shard in shards[1]]
+    qkv_w, *later = lax.optimization_barrier((qkv_w, shards[1][0], *shards[1][2:]))
+    later = [lax.all_gather(shard, everyone, axis=0, tiled=True) for shard in later]
 
     hidden = inputs.reshape(batches * tokens, D).astype(jnp.float32)
     weights_all, kept_all = [], []
@@ -1086,8 +1097,8 @@
             hidden,
             later[0] if layer else qkv_w,
             later[1:] if layer else [],
-            [] if layer else ["out", "up", "down"],
-            [] if layer else shards[0][1:],
+            ["out"] if layer else ["out", "up", "down"],
+            shards[layer][1:2] if layer else shards[0][1:],
             exchange,
             context,
             1 + layer,

time: 762 us -> 746 us (0.979)
  other arithmetic: 32.5 us -> 16.7 us
  Pallas kernels: 581 us -> 591 us
  matrix products: 83.9 us -> 74.8 us
    pallas_call x2, Pallas kernels: 198 us -> 214 us  [attention_forward(): pl.pallas_call(kernel, out_shape=[jax.ShapeDtypeStruct((held, HEAD_DIM, P...]
    convert_element_type x2, other arithmetic: 15.4 us -> 2.3 us  [layer_forward(): act_low = geglu(upper[:, :FF], upper[:, FF:]).astype(jnp.bfloat16)]
    dot_general x24, matrix products: 83.9 us -> 74.8 us  [dot(): lax.dot_general(a, b, (((a_axis,), (b_axis,)), ((), ())), preferred_eleme...]
    unnamed x194 -> x147, local copies, waits for them, and re-layouts: 15.9 us -> 13.7 us
  transfers between devices with their start and end apart: 4 -> 3, of which waited for: 0 -> 0; matrix products, arithmetic and copies ran while one was open for 7% -> 5% of each run, Pallas kernels for 31% -> 29%
where the time goes in v2:
time: 746 us; the launch traced here: 740 us
  Pallas kernels  591 us (79%)
  matrix products  74.8 us (10%)
  local copies, waits for them, and re-layouts  40.7 us (5%)
  other arithmetic  16.7 us (2%)
  between operations  15.2 us (2%)
    pallas_call x2, Pallas kernels, attention_backward(): pl.pallas_call(kernel, out_shape=[jax.ShapeDtypeStruct((held, 3 * HEAD_DI...  283 us
    pallas_call x2, Pallas kernels, attention_forward(): pl.pallas_call(kernel, out_shape=[jax.ShapeDtypeStruct((held, HEAD_DIM, P...  214 us
    pallas_call x2, Pallas kernels, run_flow(): pl.pallas_call(kernel, out_shape=flow.out_shape, in_specs=[HBM] * count,...  94.2 us
    dot_general x24, matrix products, dot(): lax.dot_general(a, b, (((a_axis,), (b_axis,)), ((), ())), preferred_eleme...  74.8 us
  transfers between devices with their start and end apart: 3, of which 0 were waited for; matrix products, arithmetic and copies ran while one was open for 5% of the time, Pallas kernels for 29%

profile of v2, /device:TPU:0, one launch (start us, length us, event | category | flops | bytes accessed | tf_op | source)
XLA Modules:
  0.0 740.0 jit_solution(10972889863562860635)
XLA Ops:
  9.1 35.9 %gather_weights.1 = bf16[2,4,2,2,24,2304]{5,4,3,2,1,0:T(8,128)(2,1)S(1)} custom-call(bf16[24,2304]{1,0:T(8,128)(2,1)S(1)} %get-tuple-element.139.refs_0_), custom_call_target="tpu_custom_call" | custom-call | bytes 110700000 | tf_op jit(solution)/shard_map/gather_weights/pallas_call | solution.py:312
  48.8 3.2 convolution_convert_fusion.7
  52.0 3.6 reshape.358
  58.8 140.2 %attention_forward.2 = (bf16[24,64,128]{2,1,0:T(8,128)(2,1)S(1)}, bf16[32,192,128]{2,1,0:T(8,128)(2,1)}, f32[32,64,128]{2,1,0:T(8,128)S(1)}, f32[16,1,256]{2,1,0...) custom-call(f32[1]{0:T(128)} %bitcast.1.slope_ref, ...), custom_call_target="tpu_custom_call" | custom-call | bytes 221400000 | tf_op jit(solution)/shard_map/attention_forward/pallas_call | solution.py:707
  205.3 5.7 fusion.71
  216.4 4.2 convolution_convert_fusion.6
  223.7 74.1 %attention_forward.3 = (bf16[24,64,128]{2,1,0:T(8,128)(2,1)S(1)}, bf16[32,192,128]{2,1,0:T(8,128)(2,1)}, f32[32,64,128]{2,1,0:T(8,128)S(1)}, f32[16,1,256]{2,1,0...) custom-call(f32[1]{0:T(128)} %bitcast.1.slope_ref, bf16[32,64,128]{2,1,0:T(8,128)(2,1)S(1)} %get-tuple-element.143.query_doc_ref, ...), custom_call_target="tpu_custom_call" | custom-call | bytes 221400000 | tf_op jit(solution)/shard_map/attention_forward/pallas_call | solution.py:707
  302.1 5.3 fusion.68
  311.6 4.3 fusion.89
  317.9 3.9 convolution_convert_fusion.5
  322.9 3.5 fusion.5
  326.5 5.7 convolution_convert_fusion.1
  332.2 2.9 multiply_reduce_fusion.4
  341.1 137.8 %attention_backward.2 = (bf16[24,192,128]{2,1,0:T(8,128)(2,1)}, f32[96,768]{1,0:T(8,128)}, f32[24,6144]{1,0:T(8,128)}, f32[24,896]{1,0:T(8,128)}) custom-call(f32[1]{0:T(128)} %bitcast.1.slope_ref, bf16[32,64,128]{2,1,0:T(8,128)(2,1)} %copy-done.4, bf16[32,64,128]{2,1,0:T(8,128)(2,1)} %copy-done.3, f32[32,64,128]{2,1,0:T(8,128)} %copy-done.9, ...), custom_call_target="tpu_custom_call" | custom-call | bytes 258300000 | tf_op jit(solution)/shard_map/attention_backward/pallas_call | solution.py:903
  481.6 3.7 multiply_reduce_fusion
  485.7 4.4 fusion.11
  490.2 3.7 convolution_convert_fusion.4
  494.0 2.9 multiply_reduce_fusion.1
  496.9 5.6 convolution_convert_fusion
  504.4 2.9 convolution_convert_fusion.3
  510.0 144.8 %attention_backward.3 = (bf16[24,192,128]{2,1,0:T(8,128)(2,1)}, f32[96,768]{1,0:T(8,128)}, f32[24,6144]{1,0:T(8,128)}, f32[24,896]{1,0:T(8,128)}) custom-call(f32[1]{0:T(128)} %bitcast.1.slope_ref, bf16[32,64,128]{2,1,0:T(8,128)(2,1)} %copy-done.4, bf16[32,64,128]{2,1,0:T(8,128)(2,1)} %copy-done.3, f32[32,64,128]{2,1,0:T(8,128)} %copy-done.8, ...), custom_call_target="tpu_custom_call" | custom-call | bytes 258300000 | tf_op jit(solution)/shard_map/attention_backward/pallas_call | solution.py:903
  657.3 3.2 convolution_add_fusion.2
  666.5 58.3 %scatter_grads.1 = (f32[24,2304]{1,0:T(8,128)S(1)}, f32[24,2304]{1,0:T(8,128)S(1)}) custom-call(bf16[2,4,2,2,24,2304]{5,4,3,2,1,0:T(8,128)(2,1)S(1)} %bitcast.126, bf16[2,4,2,2,24,2304]{5,4,3,2,1,0:T(8,128)(2,1)S(1)} %bitcast.125), custom_call_target="tpu_custom_call" | custom-call | bytes 110700000 | tf_op jit(solution)/shard_map/scatter_grads/pallas_call | solution.py:312
  728.1 2.8 fusion.75
  (251 shorter events, 62.1 us)
Async XLA Ops:
  7.2 41.4 %copy-start = (s32[2,1,8]{2,1,0:T(1,128)S(1)}, s32[2,1,8]{2,1,0:T(1,128)}, u32[]{:S(2)}) copy-start(s32[2,1,8]{2,1,0:T(1,128)} %param.20) | copy-start | bytes 196
  7.2 209.2 %all-gather.4.cloned.1.call-start = ((), (), s32[]{:S(2)}) async-start(), calls=%async_computation | async-start | bytes 3649536 | tf_op jit(solution)/shard_map/all_gather | solution.py:1091
  7.3 37.7 %copy-start.24 = (f32[2,24,6144]{2,1,0:T(8,128)S(1)}, f32[2,24,6144]{2,1,0:T(8,128)}, u32[]{:S(2)}) copy-start(f32[2,24,6144]{2,1,0:T(8,128)} %param.27) | copy-start | bytes 3538948
  9.1 36.9 %copy-start.28 = (f32[2,96,768]{2,1,0:T(8,128)S(1)}, f32[2,96,768]{2,1,0:T(8,128)}, u32[]{:S(2)}) copy-start(f32[2,96,768]{2,1,0:T(8,128)} %param.30) | copy-start | bytes 1769476
  47.0 255.1 %all-gather.6.cloned.1.call-start = ((), (), s32[]{:S(2)}) async-start(), calls=%async_computation.1 | async-start | bytes 9732096 | tf_op jit(solution)/shard_map/all_gather | solution.py:1091
  47.8 263.9 %all-gather.8.cloned.1.call-start = ((), (), s32[]{:S(2)}) async-start(), calls=%async_computation.2 | async-start | bytes 4866048 | tf_op jit(solution)/shard_map/all_gather | solution.py:1091
  58.7 164.9 %copy-start.3 = (bf16[32,64,128]{2,1,0:T(8,128)(2,1)}, bf16[32,64,128]{2,1,0:T(8,128)(2,1)S(1)}, u32[]{:S(2)}) copy-start(bf16[32,64,128]{2,1,0:T(8,128)(2,1)S(1)} %get-tuple-element.142.key_doc_ref) | copy-start | bytes 1572868
  58.7 164.9 %copy-start.4 = (bf16[32,64,128]{2,1,0:T(8,128)(2,1)}, bf16[32,64,128]{2,1,0:T(8,128)(2,1)S(1)}, u32[]{:S(2)}) copy-start(bf16[32,64,128]{2,1,0:T(8,128)(2,1)S(1)} %get-tuple-element.143.query_doc_ref) | copy-start | bytes 1572868
  201.8 9.2 %copy-start.33 = (bf16[2,768,128]{1,2,0:T(8,128)(2,1)}, bf16[2,768,128]{1,2,0:T(8,128)(2,1)S(1)}, u32[]{:S(2)}) copy-start(bf16[2,768,128]{1,2,0:T(8,128)(2,1)S(1)} %copy.70) | copy-start | bytes 1179652
  205.0 8.7 %copy-start.17 = (f32[256,768]{1,0:T(8,128)}, f32[256,768]{1,0:T(8,128)S(1)}, u32[]{:S(2)}) copy-start(f32[256,768]{1,0:T(8,128)S(1)} %get-tuple-element.145) | copy-start | bytes 2359300
  205.0 8.7 %slice-start.10 = ((s8[4718592]{0:T(1024)(128)(4,1)}), s8[4194304]{0:T(1024)(128)(4,1)S(1)}, s32[]{:S(2)}) async-start(s8[4718592]{0:T(1024)(128)(4,1)} %bitcast.182), calls=%async_computation.13 | async-start | bytes 8388608
  298.8 8.6 %copy-start.14 = (f32[16,1,256]{2,1,0:T(1,128)}, f32[16,1,256]{2,1,0:T(1,128)S(1)}, u32[]{:S(2)}) copy-start(f32[16,1,256]{2,1,0:T(1,128)S(1)} %get-tuple-element.63.sum_ref) | copy-start | bytes 49156
  322.9 9.3 %slice-start.4 = ((s8[9437184]{0:T(1024)(128)(4,1)}), s8[4194304]{0:T(1024)(128)(4,1)S(1)}, s32[]{:S(2)}) async-start(s8[9437184]{0:T(1024)(128)(4,1)} %bitcast.149), calls=%async_computation.7 | async-start | bytes 8388608
  322.9 9.3 %slice-start.5 = ((s8[9437184]{0:T(1024)(128)(4,1)}), s8[4194304]{0:T(1024)(128)(4,1)S(1)}, s32[]{:S(2)}) async-start(s8[9437184]{0:T(1024)(128)(4,1)} %bitcast.149), calls=%async_computation.8 | async-start | bytes 8388608
  341.1 140.5 %copy-start.23 = (f32[256,768]{1,0:T(8,128)S(1)}, f32[256,768]{1,0:T(8,128)}, u32[]{:S(2)}) copy-start(f32[256,768]{1,0:T(8,128)} %copy-done.22) | copy-start | bytes 2359300
  510.0 147.3 %copy-start.6 = (bf16[2,4,2,2,24,2304]{5,4,3,2,1,0:T(8,128)(2,1)S(1)}, bf16[2,4,2,2,24,2304]{5,4,3,2,1,0:T(8,128)(2,1)}, u32[]{:S(2)}) copy-start(bf16[2,4,2,2,24,2304]{5,4,3,2,1,0:T(8,128)(2,1)} %copy-done.5) | copy-start | bytes 10616836
  666.4 58.4 %copy-start.30 = (f32[2,24,2304]{2,1,0:T(8,128)S(1)}, f32[2,24,2304]{2,1,0:T(8,128)}, u32[]{:S(2)}) copy-start(f32[2,24,2304]{2,1,0:T(8,128)} %param.21) | copy-start | bytes 1327108
  666.4 58.4 %copy-start.43 = (f32[2,24,2304]{2,1,0:T(8,128)S(1)}, f32[2,24,2304]{2,1,0:T(8,128)}, u32[]{:S(2)}) copy-start(f32[2,24,2304]{2,1,0:T(8,128)} %param.23) | copy-start | bytes 1327108
  666.4 58.5 %copy-start.44 = (f32[2,24,2304]{2,1,0:T(8,128)S(1)}, f32[2,24,2304]{2,1,0:T(8,128)}, u32[]{:S(2)}) copy-start(f32[2,24,2304]{2,1,0:T(8,128)} %param.22) | copy-start | bytes 1327108
  666.4 59.9 %copy-start.42 = (f32[2,24,768]{2,1,0:T(8,128)S(1)}, f32[2,24,768]{2,1,0:T(8,128)}, u32[]{:S(2)}) copy-start(f32[2,24,768]{2,1,0:T(8,128)} %param.24) | copy-start | bytes 442372
  666.4 59.9 %copy-start.48 = (f32[1,24,768]{2,1,0:T(8,128)S(1)}, f32[1,24,768]{2,1,0:T(8,128)}, u32[]{:S(2)}) copy-start(f32[1,24,768]{2,1,0:T(8,128)} %get-tuple-element.155) | copy-start | bytes 221188
  666.4 59.8 %copy-start.49 = (f32[1,24,768]{2,1,0:T(8,128)S(1)}, f32[1,24,768]{2,1,0:T(8,128)}, u32[]{:S(2)}) copy-start(f32[1,24,768]{2,1,0:T(8,128)} %get-tuple-element.156) | copy-start | bytes 221188
  666.4 59.8 %copy-start.50 = (f32[2,24,768]{2,1,0:T(8,128)S(1)}, f32[2,24,768]{2,1,0:T(8,128)}, u32[]{:S(2)}) copy-start(f32[2,24,768]{2,1,0:T(8,128)} %param.26) | copy-start | bytes 442372
  666.5 59.8 %copy-start.51 = (f32[2,24,768]{2,1,0:T(8,128)S(1)}, f32[2,24,768]{2,1,0:T(8,128)}, u32[]{:S(2)}) copy-start(f32[2,24,768]{2,1,0:T(8,128)} %param.25) | copy-start | bytes 442372
  (51 other events, 166.1 us)
Sparse Core Ops, SparseCore 0:
  47.2 79.3 all-gather.3
  130.0 95.8 all-gather.5
  229.5 73.0 all-gather.7

commit v3 on v2

--- a/solution.py
+++ b/solution.py
@@ -103,13 +103,10 @@
     if kind == "out":
         return [halves(384, 512)]
     if kind == "up":
-        return [halves(768, 768, start) for start in range(0, 2 * FF, 1536)]
+        return [halves(384, 384, start) for start in range(0, 2 * FF, 768)]
     if rows % 32:
         return [halves(384, 384)]
-    half = rows // 2
-    return [
-        ((0, half, start, 384, ZXY), (half, half, start, 384, ZYX)) for start in range(0, D, 384)
-    ]
+    return [((row, 16, 0, D, ZXY), (row + 16, 16, 0, D, ZYX)) for row in range(0, rows, 32)]
 
 
 HBM = pl.BlockSpec(memory_space=pl.ANY)
@@ -481,8 +478,8 @@
 REACH = 2 * GUARD + 1
 DOC_ROWS = 64
 FAR = -1e30
-FORWARD_AHEAD, FORWARD_FIRST, FORWARD_LAG = 3, 5, 2
-BACKWARD_AHEAD, BACKWARD_FIRST, BACKWARD_LAG = 4, 4, 2
+FORWARD_AHEAD, FORWARD_FIRST, FORWARD_LAG = 4, 8, 2
+BACKWARD_AHEAD, BACKWARD_FIRST, BACKWARD_LAG = 5, 5, 2
 
 
 def unit_context(lengths, exchange, tokens):
@@ -958,7 +955,9 @@
 def layer_forward(hidden, qkv_w, others, kinds, shards, exchange, context, collective_id):
     batches = exchange.batches
     tokens = hidden.shape[0] // batches
-    hidden_low = lax.optimization_barrier(hidden.astype(jnp.bfloat16))
+    hidden_low = hidden.astype(jnp.bfloat16)
+    if others:
+        hidden_low = lax.optimization_barrier(hidden_low)
     packed = dot(qkv_w, hidden_low, 0, 1).astype(jnp.bfloat16)
     packed = packed.reshape(3, HEADS, HEAD_DIM, batches, tokens)
     packed = packed.transpose(3, 1, 0, 2, 4).reshape(batches * HEADS, 3 * HEAD_DIM, tokens)
@@ -968,10 +967,10 @@
         context,
         collective_id,
         Gather(kinds, shards, exchange.sizes, FORWARD_AHEAD, FORWARD_LAG),
-        FORWARD_FIRST if len(kinds) > 1 else 1,
+        FORWARD_FIRST if kinds else 0,
     )
     gathered = [one.reshape(-1, one.shape[-1]) for one in gathered]
-    out_w, up_w, down_w = gathered + others
+    out_w, up_w, down_w = others + gathered
     norm_f = out_w[:, D : D + 4].astype(jnp.float32)
     out_w = out_w[:, :D]
     attn_t = attended.reshape(batches, D, tokens)
@@ -1087,8 +1086,7 @@
     qkv_w = run_flow(Gather(["qkv"], shards[0][:1], sizes, 2, 1), 0, "gather_weights")[0]
     qkv_w = qkv_w.reshape(-1, qkv_w.shape[-1])
     everyone = ("head", "seq")
-    qkv_w, *later = lax.optimization_barrier((qkv_w, shards[1][0], *shards[1][2:]))
-    later = [lax.all_gather(shard, everyone, axis=0, tiled=True) for shard in later]
+    later = [lax.all_gather(shard, everyone, axis=0, tiled=True) for shard in shards[1]]
 
     hidden = inputs.reshape(batches * tokens, D).astype(jnp.float32)
     weights_all, kept_all = [], []
@@ -1097,8 +1095,8 @@
             hidden,
             later[0] if layer else qkv_w,
             later[1:] if layer else [],
-            ["out"] if layer else ["out", "up", "down"],
-            shards[layer][1:2] if layer else shards[0][1:],
+            [] if layer else ["out", "up", "down"],
+            [] if layer else shards[0][1:],
             exchange,
             context,
             1 + layer,

time: 746 us -> 730 us (0.979)
  Pallas kernels: 591 us -> 563 us
  waiting for transfers between devices: 1.44 us -> 9.82 us
    pallas_call x2, Pallas kernels: 214 us -> 197 us  [attention_forward(): pl.pallas_call(kernel, out_shape=[jax.ShapeDtypeStruct((held, HEAD_DIM, P...]
    pallas_call x2, Pallas kernels: 283 us -> 270 us  [attention_backward(): pl.pallas_call(kernel, out_shape=[jax.ShapeDtypeStruct((held, 3 * HEAD_DI...]
    all_gather x3 -> x4, waiting for transfers between devices: 0.04 us -> 9.75 us  [body(): lax.all_gather(shard, everyone, axis=0, tiled=True)]
    unnamed x147 -> x190, local copies, waits for them, and re-layouts: 13.7 us -> 18.2 us
  transfers between devices with their start and end apart: 3 -> 4, of which waited for: 0 -> 1; matrix products, arithmetic and copies ran while one was open for 5% -> 6% of each run, Pallas kernels for 29% -> 32%
where the time goes in v3:
time: 730 us; the launch traced here: 724 us
  Pallas kernels  563 us (77%)
  matrix products  71.5 us (10%)
  local copies, waits for them, and re-layouts  46 us (6%)
  other arithmetic  18.5 us (3%)
  between operations  15.4 us (2%)
  waiting for transfers between devices  9.82 us (1%)
    pallas_call x2, Pallas kernels, attention_backward(): pl.pallas_call(kernel, out_shape=[jax.ShapeDtypeStruct((held, 3 * HEAD_DI...  270 us
    pallas_call x2, Pallas kernels, attention_forward(): pl.pallas_call(kernel, out_shape=[jax.ShapeDtypeStruct((held, HEAD_DIM, P...  197 us
    pallas_call x2, Pallas kernels, run_flow(): pl.pallas_call(kernel, out_shape=flow.out_shape, in_specs=[HBM] * count,...  95.5 us
    dot_general x24, matrix products, dot(): lax.dot_general(a, b, (((a_axis,), (b_axis,)), ((), ())), preferred_eleme...  71.5 us
    unnamed x190, local copies, waits for them, and re-layouts  18.2 us
  transfers between devices with their start and end apart: 4, of which 1 were waited for; matrix products, arithmetic and copies ran while one was open for 6% of the time, Pallas kernels for 32%

profile of v3, /device:TPU:0, one launch (start us, length us, event | category | flops | bytes accessed | tf_op | source)
XLA Modules:
  0.0 724.0 jit_solution(16164768448572137578)
XLA Ops:
  14.7 36.9 %gather_weights.1 = bf16[2,4,2,2,24,2304]{5,4,3,2,1,0:T(8,128)(2,1)S(1)} custom-call(bf16[24,2304]{1,0:T(8,128)(2,1)S(1)} %get-tuple-element.129.refs_0_), custom_call_target="tpu_custom_call" | custom-call | bytes 110700000 | tf_op jit(solution)/shard_map/gather_weights/pallas_call | solution.py:309
  55.7 132.1 %attention_forward.2 = (bf16[24,64,128]{2,1,0:T(8,128)(2,1)S(1)}, bf16[32,192,128]{2,1,0:T(8,128)(2,1)}, f32[32,64,128]{2,1,0:T(8,128)S(1)}, f32[16,1,256]{2,1,0...) custom-call(f32[1]{0:T(128)} %bitcast.1.slope_ref, ...), custom_call_target="tpu_custom_call" | custom-call | bytes 221400000 | tf_op jit(solution)/shard_map/attention_forward/pallas_call | solution.py:704
  194.2 5.5 fusion.88
  207.2 4.2 fusion.8
  213.8 3.6 reshape.362
  218.9 64.9 %attention_forward.3 = (bf16[24,64,128]{2,1,0:T(8,128)(2,1)S(1)}, bf16[32,192,128]{2,1,0:T(8,128)(2,1)S(1)}, f32[32,64,128]{2,1,0:T(8,128)S(1)}, f32[16,1,256]{2,1,0:T(1,128)S(1)}) custom-call(f32[1]{0:T(128)} %bitcast.1.slope_ref, bf16[32,64,128]{2,1,0:T(8,128)(2,1)S(1)} %get-tuple-element.133.query_doc_ref, ...), custom_call_target="tpu_custom_call" | custom-call | bytes 221400000 | tf_op jit(solution)/shard_map/attention_forward/pallas_call | solution.py:704
  290.4 5.3 fusion.2
  299.1 9.7 %all-gather.15.cloned.1.call-done = bf16[1,3072,768]{2,1,0:T(8,128)(2,1)} async-done(((bf16[1,96,768]{2,1,0:T(8,128)(2,1)}), bf16[1,3072,768]{2,1,0:T(8,128)(2,1)}) %all-gather.15.cloned.1.call-update) | async-done | bytes 4718608 | tf_op jit(solution)/shard_map/all_gather | solution.py:1089
  308.8 3.9 fusion.109
  315.2 3.9 convolution_convert_fusion.5
  320.4 3.5 fusion.17
  323.9 5.8 convolution_convert_fusion.1
  329.8 2.9 multiply_reduce_fusion.4
  337.3 127.8 %attention_backward.2 = (bf16[24,192,128]{2,1,0:T(8,128)(2,1)}, f32[96,768]{1,0:T(8,128)}, f32[24,6144]{1,0:T(8,128)}, f32[24,896]{1,0:T(8,128)}) custom-call(f32[1]{0:T(128)} %bitcast.1.slope_ref, bf16[32,64,128]{2,1,0:T(8,128)(2,1)} %copy-done.4, bf16[32,64,128]{2,1,0:T(8,128)(2,1)} %copy-done.3, f32[32,64,128]{2,1,0:T(8,128)} %copy-done.9, ...), custom_call_target="tpu_custom_call" | custom-call | bytes 258300000 | tf_op jit(solution)/shard_map/attention_backward/pallas_call | solution.py:900
  467.9 3.7 multiply_reduce_fusion
  472.0 4.4 fusion.23
  476.5 3.7 convolution_convert_fusion.4
  480.3 2.9 multiply_reduce_fusion.1
  483.2 5.5 convolution_convert_fusion
  490.6 2.9 convolution_convert_fusion.3
  496.3 142.2 %attention_backward.3 = (bf16[24,192,128]{2,1,0:T(8,128)(2,1)}, f32[96,768]{1,0:T(8,128)}, f32[24,6144]{1,0:T(8,128)}, f32[24,896]{1,0:T(8,128)}) custom-call(f32[1]{0:T(128)} %bitcast.1.slope_ref, bf16[32,64,128]{2,1,0:T(8,128)(2,1)} %copy-done.4, bf16[32,64,128]{2,1,0:T(8,128)(2,1)} %copy-done.3, f32[32,64,128]{2,1,0:T(8,128)} %copy-done.8, ...), custom_call_target="tpu_custom_call" | custom-call | bytes 258300000 | tf_op jit(solution)/shard_map/attention_backward/pallas_call | solution.py:900
  641.0 3.2 convolution_add_fusion.2
  650.2 58.6 %scatter_grads.1 = (f32[24,2304]{1,0:T(8,128)S(1)}, f32[24,2304]{1,0:T(8,128)S(1)}) custom-call(bf16[2,4,2,2,24,2304]{5,4,3,2,1,0:T(8,128)(2,1)S(1)} %bitcast.142, bf16[2,4,2,2,24,2304]{5,4,3,2,1,0:T(8,128)(2,1)S(1)} %bitcast.141), custom_call_target="tpu_custom_call" | custom-call | bytes 110700000 | tf_op jit(solution)/shard_map/scatter_grads/pallas_call | solution.py:309
  712.1 2.8 fusion.92
  (297 shorter events, 68.4 us)
Async XLA Ops:
  7.2 197.9 %all-gather.11.cloned.1.call-start = ((), (), s32[]{:S(2)}) async-start(), calls=%async_computation.1 | async-start | bytes 1419264 | tf_op jit(solution)/shard_map/all_gather | solution.py:1089
  9.7 197.6 %all-gather.9.cloned.1.call-start = ((), (), s32[]{:S(2)}) async-start(), calls=%async_computation | async-start | bytes 3649536 | tf_op jit(solution)/shard_map/all_gather | solution.py:1089
  11.5 278.4 %all-gather.13.cloned.1.call-start = ((), (), s32[]{:S(2)}) async-start(), calls=%async_computation.2 | async-start | bytes 9732096 | tf_op jit(solution)/shard_map/all_gather | solution.py:1089
  13.6 295.2 %all-gather.15.cloned.1.call-start = ((), (), s32[]{:S(2)}) async-start(), calls=%async_computation.3 | async-start | bytes 4866048 | tf_op jit(solution)/shard_map/all_gather | solution.py:1089
  55.7 163.2 %copy-start.3 = (bf16[32,64,128]{2,1,0:T(8,128)(2,1)}, bf16[32,64,128]{2,1,0:T(8,128)(2,1)S(1)}, u32[]{:S(2)}) copy-start(bf16[32,64,128]{2,1,0:T(8,128)(2,1)S(1)} %get-tuple-element.132.key_doc_ref) | copy-start | bytes 1572868
  55.7 163.2 %copy-start.4 = (bf16[32,64,128]{2,1,0:T(8,128)(2,1)}, bf16[32,64,128]{2,1,0:T(8,128)(2,1)S(1)}, u32[]{:S(2)}) copy-start(bf16[32,64,128]{2,1,0:T(8,128)(2,1)S(1)} %get-tuple-element.133.query_doc_ref) | copy-start | bytes 1572868
  192.0 95.6 %copy-start.61 = (f32[768]{0:T(1024)}, f32[768]{0:T(1024)S(1)}, u32[]{:S(2)}) copy-start(f32[768]{0:T(1024)S(1)} %get-tuple-element.83) | copy-start | bytes 9220
  203.9 83.7 %copy-start.18 = (f32[256,768]{1,0:T(8,128)}, f32[256,768]{1,0:T(8,128)S(1)}, u32[]{:S(2)}) copy-start(f32[256,768]{1,0:T(8,128)S(1)} %get-tuple-element.137) | copy-start | bytes 2359300
  203.9 83.7 %copy-start.65 = (f32[256]{0:T(256)}, f32[256]{0:T(256)S(1)}, u32[]{:S(2)}) copy-start(f32[256]{0:T(256)S(1)} %broadcast_multiply_fusion.2) | copy-start | bytes 3076
  204.1 83.4 %copy-start.69 = (f32[256]{0:T(256)}, f32[256]{0:T(256)S(1)}, u32[]{:S(2)}) copy-start(f32[256]{0:T(256)S(1)} %fusion.77) | copy-start | bytes 3076
  337.3 130.5 %copy-start.19 = (f32[256,768]{1,0:T(8,128)S(1)}, f32[256,768]{1,0:T(8,128)}, u32[]{:S(2)}) copy-start(f32[256,768]{1,0:T(8,128)} %copy-done.18) | copy-start | bytes 2359300
  337.3 130.5 %copy-start.24 = (f32[256,768]{1,0:T(8,128)S(1)}, f32[256,768]{1,0:T(8,128)}, u32[]{:S(2)}) copy-start(f32[256,768]{1,0:T(8,128)} %copy-done.23) | copy-start | bytes 2359300
  337.3 130.5 %copy-start.62 = (f32[768]{0:T(1024)S(1)}, f32[768]{0:T(1024)}, u32[]{:S(2)}) copy-start(f32[768]{0:T(1024)} %copy-done.61) | copy-start | bytes 9220
  337.3 130.5 %copy-start.66 = (f32[256]{0:T(256)S(1)}, f32[256]{0:T(256)}, u32[]{:S(2)}) copy-start(f32[256]{0:T(256)} %copy-done.65) | copy-start | bytes 3076
  337.3 130.5 %copy-start.70 = (f32[256]{0:T(256)S(1)}, f32[256]{0:T(256)}, u32[]{:S(2)}) copy-start(f32[256]{0:T(256)} %copy-done.69) | copy-start | bytes 3076
  496.3 144.7 %copy-start.6 = (bf16[2,4,2,2,24,2304]{5,4,3,2,1,0:T(8,128)(2,1)S(1)}, bf16[2,4,2,2,24,2304]{5,4,3,2,1,0:T(8,128)(2,1)}, u32[]{:S(2)}) copy-start(bf16[2,4,2,2,24,2304]{5,4,3,2,1,0:T(8,128)(2,1)} %copy-done.5) | copy-start | bytes 10616836
  650.1 58.7 %copy-start.27 = (f32[2,24,2304]{2,1,0:T(8,128)S(1)}, f32[2,24,2304]{2,1,0:T(8,128)}, u32[]{:S(2)}) copy-start(f32[2,24,2304]{2,1,0:T(8,128)} %param.21) | copy-start | bytes 1327108
  650.1 58.7 %copy-start.42 = (f32[2,24,2304]{2,1,0:T(8,128)S(1)}, f32[2,24,2304]{2,1,0:T(8,128)}, u32[]{:S(2)}) copy-start(f32[2,24,2304]{2,1,0:T(8,128)} %param.23) | copy-start | bytes 1327108
  650.1 58.7 %copy-start.43 = (f32[2,24,2304]{2,1,0:T(8,128)S(1)}, f32[2,24,2304]{2,1,0:T(8,128)}, u32[]{:S(2)}) copy-start(f32[2,24,2304]{2,1,0:T(8,128)} %param.22) | copy-start | bytes 1327108
  650.1 60.1 %copy-start.39 = (f32[2,24,768]{2,1,0:T(8,128)S(1)}, f32[2,24,768]{2,1,0:T(8,128)}, u32[]{:S(2)}) copy-start(f32[2,24,768]{2,1,0:T(8,128)} %param.24) | copy-start | bytes 442372
  650.1 60.1 %copy-start.48 = (f32[1,24,768]{2,1,0:T(8,128)S(1)}, f32[1,24,768]{2,1,0:T(8,128)}, u32[]{:S(2)}) copy-start(f32[1,24,768]{2,1,0:T(8,128)} %get-tuple-element.145) | copy-start | bytes 221188
  650.1 60.1 %copy-start.49 = (f32[1,24,768]{2,1,0:T(8,128)S(1)}, f32[1,24,768]{2,1,0:T(8,128)}, u32[]{:S(2)}) copy-start(f32[1,24,768]{2,1,0:T(8,128)} %get-tuple-element.146) | copy-start | bytes 221188
  650.2 60.1 %copy-start.50 = (f32[2,24,768]{2,1,0:T(8,128)S(1)}, f32[2,24,768]{2,1,0:T(8,128)}, u32[]{:S(2)}) copy-start(f32[2,24,768]{2,1,0:T(8,128)} %param.26) | copy-start | bytes 442372
  650.2 60.1 %copy-start.51 = (f32[2,24,768]{2,1,0:T(8,128)S(1)}, f32[2,24,768]{2,1,0:T(8,128)}, u32[]{:S(2)}) copy-start(f32[2,24,768]{2,1,0:T(8,128)} %param.25) | copy-start | bytes 442372
  (74 other events, 322.2 us)
Sparse Core Ops, SparseCore 0:
  11.5 59.1 all-gather.10
  74.2 73.6 all-gather.8
  151.4 83.7 all-gather.12
  238.5 70.3 all-gather.14

commit v4 on v3

--- a/solution.py
+++ b/solution.py
@@ -5,6 +5,7 @@
 import jax.numpy as jnp
 from jax import lax
 from jax.experimental import pallas as pl
+from jax.experimental.layout import Layout, with_layout_constraint
 from jax.experimental.pallas import tpu as pltpu
 from jax.sharding import PartitionSpec as P
 
@@ -479,7 +480,7 @@
 DOC_ROWS = 64
 FAR = -1e30
 FORWARD_AHEAD, FORWARD_FIRST, FORWARD_LAG = 4, 8, 2
-BACKWARD_AHEAD, BACKWARD_FIRST, BACKWARD_LAG = 5, 5, 2
+BACKWARD_AHEAD, BACKWARD_FIRST, BACKWARD_LAG = 8, 5, 2
 
 
 def unit_context(lengths, exchange, tokens):
@@ -956,9 +957,8 @@
     batches = exchange.batches
     tokens = hidden.shape[0] // batches
     hidden_low = hidden.astype(jnp.bfloat16)
-    if others:
-        hidden_low = lax.optimization_barrier(hidden_low)
     packed = dot(qkv_w, hidden_low, 0, 1).astype(jnp.bfloat16)
+    packed = with_layout_constraint(packed, Layout((0, 1)))
     packed = packed.reshape(3, HEADS, HEAD_DIM, batches, tokens)
     packed = packed.transpose(3, 1, 0, 2, 4).reshape(batches * HEADS, 3 * HEAD_DIM, tokens)
     attended, unit_packed, wide, sums, *gathered = attention_forward(
@@ -1086,7 +1086,9 @@
     qkv_w = run_flow(Gather(["qkv"], shards[0][:1], sizes, 2, 1), 0, "gather_weights")[0]
     qkv_w = qkv_w.reshape(-1, qkv_w.shape[-1])
     everyone = ("head", "seq")
-    later = [lax.all_gather(shard, everyone, axis=0, tiled=True) for shard in shards[1]]
+    later = [jnp.concatenate(shards[1][:2], axis=1)] + shards[1][2:]
+    later = [lax.all_gather(shard, everyone, axis=0, tiled=True) for shard in later]
+    later = [later[0][:, : 3 * D], later[0][:, 3 * D :]] + later[1:]
 
     hidden = inputs.reshape(batches * tokens, D).astype(jnp.float32)
     weights_all, kept_all = [], []
@@ -1118,7 +1120,7 @@
         )
         totals[layer][3], totals[layer][2], totals[layer][1] = done
         late.append(grad_qkv_w)
-    last = Scatter(["qkv"] * LAYERS, late, sizes, 4, 2)
+    last = Scatter(["qkv"] * LAYERS, late, sizes, 6, 2)
     totals[1][0], totals[0][0] = run_flow(last, 1 + 2 * LAYERS, "scatter_grads")
     input_grad = grad_hidden.reshape(batches, tokens, D)
 

time: 730 us -> 772 us (1.058)
  Pallas kernels: 563 us -> 617 us
  waiting for transfers between devices: 9.82 us -> 0.11 us
    pallas_call x2, Pallas kernels: 197 us -> 226 us  [attention_forward(): pl.pallas_call(kernel, out_shape=[jax.ShapeDtypeStruct((held, HEAD_DIM, P...]
    pallas_call x2, Pallas kernels: 270 us -> 291 us  [attention_backward(): pl.pallas_call(kernel, out_shape=[jax.ShapeDtypeStruct((held, 3 * HEAD_DI...]
    all_gather x4 -> x3, waiting for transfers between devices: 9.75 us -> 0.06 us  [body(): lax.all_gather(shard, everyone, axis=0, tiled=True)]
  transfers between devices with their start and end apart: 4 -> 3, of which waited for: 1 -> 0; matrix products, arithmetic and copies ran while one was open for 6% -> 5% of each run, Pallas kernels for 32% -> 34%
where the time goes in v4:
time: 772 us; the launch traced here: 767 us
  Pallas kernels  617 us (80%)
  matrix products  73 us (9%)
  local copies, waits for them, and re-layouts  40.9 us (5%)
  other arithmetic  20.2 us (3%)
  between operations  15.5 us (2%)
    pallas_call x2, Pallas kernels, attention_backward(): pl.pallas_call(kernel, out_shape=[jax.ShapeDtypeStruct((held, 3 * HEAD_DI...  291 us
    pallas_call x2, Pallas kernels, attention_forward(): pl.pallas_call(kernel, out_shape=[jax.ShapeDtypeStruct((held, HEAD_DIM, P...  226 us
    pallas_call x2, Pallas kernels, run_flow(): pl.pallas_call(kernel, out_shape=flow.out_shape, in_specs=[HBM] * count,...  100 us
    dot_general x24, matrix products, dot(): lax.dot_general(a, b, (((a_axis,), (b_axis,)), ((), ())), preferred_eleme...  73 us
    unnamed x190, local copies, waits for them, and re-layouts  17.6 us
  transfers between devices with their start and end apart: 3, of which 0 were waited for; matrix products, arithmetic and copies ran while one was open for 5% of the time, Pallas kernels for 34%

profile of v4, /device:TPU:0, one launch (start us, length us, event | category | flops | bytes accessed | tf_op | source)
XLA Modules:
  0.0 766.6 jit_solution(1749833928908876692)
XLA Ops:
  14.1 37.9 %gather_weights.1 = bf16[2,4,2,2,24,2304]{5,4,3,2,1,0:T(8,128)(2,1)S(1)} custom-call(bf16[24,2304]{1,0:T(8,128)(2,1)S(1)} %get-tuple-element.128.refs_0_), custom_call_target="tpu_custom_call" | custom-call | bytes 110700000 | tf_op jit(solution)/shard_map/gather_weights/pallas_call | solution.py:310
  56.1 157.5 %attention_forward.2 = (bf16[24,64,128]{2,1,0:T(8,128)(2,1)S(1)}, bf16[32,192,128]{2,1,0:T(8,128)(2,1)}, f32[32,64,128]{2,1,0:T(8,128)S(1)}, f32[16,1,256]{2,1,0...) custom-call(f32[1]{0:T(128)} %bitcast.1.slope_ref, ...), custom_call_target="tpu_custom_call" | custom-call | bytes 221400000 | tf_op jit(solution)/shard_map/attention_forward/pallas_call | solution.py:705
  221.6 5.5 fusion.89
  231.6 4.3 convolution_convert_fusion.6
  235.9 3.5 reshape.362
  241.0 68.2 %attention_forward.3 = (bf16[24,64,128]{2,1,0:T(8,128)(2,1)S(1)}, bf16[32,192,128]{2,1,0:T(8,128)(2,1)S(1)}, f32[32,64,128]{2,1,0:T(8,128)S(1)}, f32[16,1,256]{2,1,0:T(1,128)S(1)}) custom-call(f32[1]{0:T(128)} %bitcast.1.slope_ref, bf16[32,64,128]{2,1,0:T(8,128)(2,1)S(1)} %get-tuple-element.133.query_doc_ref, ...), custom_call_target="tpu_custom_call" | custom-call | bytes 221400000 | tf_op jit(solution)/shard_map/attention_forward/pallas_call | solution.py:705
  316.7 5.4 fusion.2
  322.1 2.6 copy-done.15
  325.5 3.9 fusion.108
  331.9 3.9 convolution_convert_fusion.5
  337.1 3.5 fusion.13
  340.7 5.7 convolution_convert_fusion.1
  346.4 2.9 multiply_reduce_fusion.4
  355.2 144.5 %attention_backward.2 = (bf16[24,192,128]{2,1,0:T(8,128)(2,1)}, f32[96,768]{1,0:T(8,128)}, f32[24,6144]{1,0:T(8,128)}, f32[24,896]{1,0:T(8,128)}) custom-call(f32[1]{0:T(128)} %bitcast.1.slope_ref, bf16[32,64,128]{2,1,0:T(8,128)(2,1)} %copy-done.4, bf16[32,64,128]{2,1,0:T(8,128)(2,1)} %copy-done.3, f32[32,64,128]{2,1,0:T(8,128)} %copy-done.9, ...), custom_call_target="tpu_custom_call" | custom-call | bytes 258300000 | tf_op jit(solution)/shard_map/attention_backward/pallas_call | solution.py:901
  502.4 3.7 multiply_reduce_fusion
  506.5 4.4 fusion.19
  511.0 3.7 convolution_convert_fusion.4
  514.8 2.9 multiply_reduce_fusion.1
  517.7 5.7 convolution_convert_fusion
  525.3 3.1 convolution_convert_fusion.3
  531.0 146.6 %attention_backward.3 = (bf16[24,192,128]{2,1,0:T(8,128)(2,1)}, f32[96,768]{1,0:T(8,128)}, f32[24,6144]{1,0:T(8,128)}, f32[24,896]{1,0:T(8,128)}) custom-call(f32[1]{0:T(128)} %bitcast.1.slope_ref, bf16[32,64,128]{2,1,0:T(8,128)(2,1)} %copy-done.4, bf16[32,64,128]{2,1,0:T(8,128)(2,1)} %copy-done.3, f32[32,64,128]{2,1,0:T(8,128)} %copy-done.8, ...), custom_call_target="tpu_custom_call" | custom-call | bytes 258300000 | tf_op jit(solution)/shard_map/attention_backward/pallas_call | solution.py:901
  680.1 3.2 convolution_add_fusion.2
  689.3 62.1 %scatter_grads.1 = (f32[24,2304]{1,0:T(8,128)S(1)}, f32[24,2304]{1,0:T(8,128)S(1)}) custom-call(bf16[2,4,2,2,24,2304]{5,4,3,2,1,0:T(8,128)(2,1)S(1)} %bitcast.133, bf16[2,4,2,2,24,2304]{5,4,3,2,1,0:T(8,128)(2,1)S(1)} %bitcast.132), custom_call_target="tpu_custom_call" | custom-call | bytes 110700000 | tf_op jit(solution)/shard_map/scatter_grads/pallas_call | solution.py:310
  754.7 2.8 fusion.93
  (293 shorter events, 63.5 us)
Async XLA Ops:
  7.2 224.4 %all-gather.6.cloned.1.call-start = ((), (), s32[]{:S(2)}) async-start(), calls=%async_computation | async-start | bytes 5068800 | tf_op jit(solution)/shard_map/all_gather | solution.py:1090
  10.8 305.9 %all-gather.8.cloned.1.call-start = ((), (), s32[]{:S(2)}) async-start(), calls=%async_computation.1 | async-start | bytes 9732096 | tf_op jit(solution)/shard_map/all_gather | solution.py:1090
  13.0 312.5 %all-gather.10.cloned.1.call-start = ((), (), s32[]{:S(2)}) async-start(), calls=%async_computation.2 | async-start | bytes 4866048 | tf_op jit(solution)/shard_map/all_gather | solution.py:1090
  56.0 185.0 %copy-start.3 = (bf16[32,64,128]{2,1,0:T(8,128)(2,1)}, bf16[32,64,128]{2,1,0:T(8,128)(2,1)S(1)}, u32[]{:S(2)}) copy-start(bf16[32,64,128]{2,1,0:T(8,128)(2,1)S(1)} %get-tuple-element.132.key_doc_ref) | copy-start | bytes 1572868
  56.0 185.0 %copy-start.4 = (bf16[32,64,128]{2,1,0:T(8,128)(2,1)}, bf16[32,64,128]{2,1,0:T(8,128)(2,1)S(1)}, u32[]{:S(2)}) copy-start(bf16[32,64,128]{2,1,0:T(8,128)(2,1)S(1)} %get-tuple-element.133.query_doc_ref) | copy-start | bytes 1572868
  219.4 95.1 %copy-start.60 = (f32[768]{0:T(1024)}, f32[768]{0:T(1024)S(1)}, u32[]{:S(2)}) copy-start(f32[768]{0:T(1024)S(1)} %get-tuple-element.83) | copy-start | bytes 9220
  219.4 95.1 %copy-start.65 = (f32[768]{0:T(1024)}, f32[768]{0:T(1024)S(1)}, u32[]{:S(2)}) copy-start(f32[768]{0:T(1024)S(1)} %get-tuple-element.84) | copy-start | bytes 9220
  231.3 83.2 %copy-start.18 = (f32[256,768]{1,0:T(8,128)}, f32[256,768]{1,0:T(8,128)S(1)}, u32[]{:S(2)}) copy-start(f32[256,768]{1,0:T(8,128)S(1)} %get-tuple-element.137) | copy-start | bytes 2359300
  231.3 83.2 %copy-start.63 = (f32[256]{0:T(256)}, f32[256]{0:T(256)S(1)}, u32[]{:S(2)}) copy-start(f32[256]{0:T(256)S(1)} %broadcast_multiply_fusion.2) | copy-start | bytes 3076
  231.6 82.9 %copy-start.69 = (f32[256]{0:T(256)}, f32[256]{0:T(256)S(1)}, u32[]{:S(2)}) copy-start(f32[256]{0:T(256)S(1)} %fusion.76) | copy-start | bytes 3076
  355.1 147.2 %copy-start.19 = (f32[256,768]{1,0:T(8,128)S(1)}, f32[256,768]{1,0:T(8,128)}, u32[]{:S(2)}) copy-start(f32[256,768]{1,0:T(8,128)} %copy-done.18) | copy-start | bytes 2359300
  355.1 147.2 %copy-start.24 = (f32[256,768]{1,0:T(8,128)S(1)}, f32[256,768]{1,0:T(8,128)}, u32[]{:S(2)}) copy-start(f32[256,768]{1,0:T(8,128)} %copy-done.23) | copy-start | bytes 2359300
  355.1 147.2 %copy-start.61 = (f32[768]{0:T(1024)S(1)}, f32[768]{0:T(1024)}, u32[]{:S(2)}) copy-start(f32[768]{0:T(1024)} %copy-done.60) | copy-start | bytes 9220
  355.1 147.2 %copy-start.64 = (f32[256]{0:T(256)S(1)}, f32[256]{0:T(256)}, u32[]{:S(2)}) copy-start(f32[256]{0:T(256)} %copy-done.63) | copy-start | bytes 3076
  355.1 147.2 %copy-start.70 = (f32[256]{0:T(256)S(1)}, f32[256]{0:T(256)}, u32[]{:S(2)}) copy-start(f32[256]{0:T(256)} %copy-done.69) | copy-start | bytes 3076
  531.0 149.1 %copy-start.6 = (bf16[2,4,2,2,24,2304]{5,4,3,2,1,0:T(8,128)(2,1)S(1)}, bf16[2,4,2,2,24,2304]{5,4,3,2,1,0:T(8,128)(2,1)}, u32[]{:S(2)}) copy-start(bf16[2,4,2,2,24,2304]{5,4,3,2,1,0:T(8,128)(2,1)} %copy-done.5) | copy-start | bytes 10616836
  689.2 62.2 %copy-start.27 = (f32[2,24,2304]{2,1,0:T(8,128)S(1)}, f32[2,24,2304]{2,1,0:T(8,128)}, u32[]{:S(2)}) copy-start(f32[2,24,2304]{2,1,0:T(8,128)} %param.21) | copy-start | bytes 1327108
  689.2 62.2 %copy-start.39 = (f32[2,24,2304]{2,1,0:T(8,128)S(1)}, f32[2,24,2304]{2,1,0:T(8,128)}, u32[]{:S(2)}) copy-start(f32[2,24,2304]{2,1,0:T(8,128)} %param.23) | copy-start | bytes 1327108
  689.2 62.3 %copy-start.40 = (f32[2,24,2304]{2,1,0:T(8,128)S(1)}, f32[2,24,2304]{2,1,0:T(8,128)}, u32[]{:S(2)}) copy-start(f32[2,24,2304]{2,1,0:T(8,128)} %param.22) | copy-start | bytes 1327108
  689.2 63.7 %copy-start.38 = (f32[2,24,768]{2,1,0:T(8,128)S(1)}, f32[2,24,768]{2,1,0:T(8,128)}, u32[]{:S(2)}) copy-start(f32[2,24,768]{2,1,0:T(8,128)} %param.24) | copy-start | bytes 442372
  689.2 63.7 %copy-start.45 = (f32[1,24,768]{2,1,0:T(8,128)S(1)}, f32[1,24,768]{2,1,0:T(8,128)}, u32[]{:S(2)}) copy-start(f32[1,24,768]{2,1,0:T(8,128)} %get-tuple-element.145) | copy-start | bytes 221188
  689.2 63.6 %copy-start.46 = (f32[1,24,768]{2,1,0:T(8,128)S(1)}, f32[1,24,768]{2,1,0:T(8,128)}, u32[]{:S(2)}) copy-start(f32[1,24,768]{2,1,0:T(8,128)} %get-tuple-element.146) | copy-start | bytes 221188
  689.2 63.6 %copy-start.47 = (f32[2,24,768]{2,1,0:T(8,128)S(1)}, f32[2,24,768]{2,1,0:T(8,128)}, u32[]{:S(2)}) copy-start(f32[2,24,768]{2,1,0:T(8,128)} %param.26) | copy-start | bytes 442372
  689.2 63.6 %copy-start.48 = (f32[2,24,768]{2,1,0:T(8,128)S(1)}, f32[2,24,768]{2,1,0:T(8,128)}, u32[]{:S(2)}) copy-start(f32[2,24,768]{2,1,0:T(8,128)} %param.25) | copy-start | bytes 442372
  (73 other events, 326.9 us)
Sparse Core Ops, SparseCore 0:
  11.5 86.9 all-gather.5
  102.0 111.7 all-gather.7
  217.2 83.6 all-gather.9

commit v5 on v4

--- a/solution.py
+++ b/solution.py
@@ -479,8 +479,8 @@
 REACH = 2 * GUARD + 1
 DOC_ROWS = 64
 FAR = -1e30
-FORWARD_AHEAD, FORWARD_FIRST, FORWARD_LAG = 4, 8, 2
-BACKWARD_AHEAD, BACKWARD_FIRST, BACKWARD_LAG = 8, 5, 2
+FORWARD_AHEAD, FORWARD_FIRST, FORWARD_LAG = 2, 8, 2
+BACKWARD_AHEAD, BACKWARD_FIRST, BACKWARD_LAG = 2, 5, 2
 
 
 def unit_context(lengths, exchange, tokens):
@@ -1086,9 +1086,7 @@
     qkv_w = run_flow(Gather(["qkv"], shards[0][:1], sizes, 2, 1), 0, "gather_weights")[0]
     qkv_w = qkv_w.reshape(-1, qkv_w.shape[-1])
     everyone = ("head", "seq")
-    later = [jnp.concatenate(shards[1][:2], axis=1)] + shards[1][2:]
-    later = [lax.all_gather(shard, everyone, axis=0, tiled=True) for shard in later]
-    later = [later[0][:, : 3 * D], later[0][:, 3 * D :]] + later[1:]
+    later = [lax.all_gather(shard, everyone, axis=0, tiled=True) for shard in shards[1]]
 
     hidden = inputs.reshape(batches * tokens, D).astype(jnp.float32)
     weights_all, kept_all = [], []
@@ -1120,7 +1118,7 @@
         )
         totals[layer][3], totals[layer][2], totals[layer][1] = done
         late.append(grad_qkv_w)
-    last = Scatter(["qkv"] * LAYERS, late, sizes, 6, 2)
+    last = Scatter(["qkv"] * LAYERS, late, sizes, 2, 2)
     totals[1][0], totals[0][0] = run_flow(last, 1 + 2 * LAYERS, "scatter_grads")
     input_grad = grad_hidden.reshape(batches, tokens, D)
 

time: 772 us -> 741 us (0.960)
  Pallas kernels: 617 us -> 564 us
  waiting for transfers between devices: 0.11 us -> 21.7 us
    pallas_call x2, Pallas kernels: 226 us -> 197 us  [attention_forward(): pl.pallas_call(kernel, out_shape=[jax.ShapeDtypeStruct((held, HEAD_DIM, P...]
    all_gather x3 -> x4, waiting for transfers between devices: 0.06 us -> 21.6 us  [body(): lax.all_gather(shard, everyone, axis=0, tiled=True)]
    pallas_call x2, Pallas kernels: 291 us -> 271 us  [attention_backward(): pl.pallas_call(kernel, out_shape=[jax.ShapeDtypeStruct((held, 3 * HEAD_DI...]
    unnamed x190 -> x192, local copies, waits for them, and re-layouts: 17.6 us -> 17.8 us
  transfers between devices with their start and end apart: 3 -> 4, of which waited for: 0 -> 1; matrix products, arithmetic and copies ran while one was open for 5% -> 6% of each run, Pallas kernels for 34% -> 32%
where the time goes in v5:
time: 741 us; the launch traced here: 735 us
  Pallas kernels  564 us (76%)
  matrix products  72.2 us (10%)
  local copies, waits for them, and re-layouts  42.4 us (6%)
  waiting for transfers between devices  21.7 us (3%)
  other arithmetic  19.3 us (3%)
  between operations  15.5 us (2%)
    pallas_call x2, Pallas kernels, attention_backward(): pl.pallas_call(kernel, out_shape=[jax.ShapeDtypeStruct((held, 3 * HEAD_DI...  271 us
    pallas_call x2, Pallas kernels, attention_forward(): pl.pallas_call(kernel, out_shape=[jax.ShapeDtypeStruct((held, HEAD_DIM, P...  197 us
    pallas_call x2, Pallas kernels, run_flow(): pl.pallas_call(kernel, out_shape=flow.out_shape, in_specs=[HBM] * count,...  95.7 us
    dot_general x24, matrix products, dot(): lax.dot_general(a, b, (((a_axis,), (b_axis,)), ((), ())), preferred_eleme...  72.2 us
    all_gather x4, waiting for transfers between devices, body(): lax.all_gather(shard, everyone, axis=0, tiled=True)  21.6 us
    unnamed x192, local copies, waits for them, and re-layouts  17.8 us
  transfers between devices with their start and end apart: 4, of which 1 were waited for; matrix products, arithmetic and copies ran while one was open for 6% of the time, Pallas kernels for 32%

profile of v5, /device:TPU:0, one launch (start us, length us, event | category | flops | bytes accessed | tf_op | source)
XLA Modules:
  0.0 735.0 jit_solution(2217354791972722208)
XLA Ops:
  14.7 36.9 %gather_weights.1 = bf16[2,4,2,2,24,2304]{5,4,3,2,1,0:T(8,128)(2,1)S(1)} custom-call(bf16[24,2304]{1,0:T(8,128)(2,1)S(1)} %get-tuple-element.128.refs_0_), custom_call_target="tpu_custom_call" | custom-call | bytes 110700000 | tf_op jit(solution)/shard_map/gather_weights/pallas_call | solution.py:310
  55.7 132.3 %attention_forward.2 = (bf16[24,64,128]{2,1,0:T(8,128)(2,1)S(1)}, bf16[32,192,128]{2,1,0:T(8,128)(2,1)}, f32[32,64,128]{2,1,0:T(8,128)S(1)}, f32[16,1,256]{2,1,0...) custom-call(f32[1]{0:T(128)} %bitcast.1.slope_ref, ...), custom_call_target="tpu_custom_call" | custom-call | bytes 221400000 | tf_op jit(solution)/shard_map/attention_forward/pallas_call | solution.py:705
  196.1 5.5 fusion.90
  208.3 4.7 fusion.8
  213.0 3.5 reshape.362
  218.1 64.7 %attention_forward.3 = (bf16[24,64,128]{2,1,0:T(8,128)(2,1)S(1)}, bf16[32,192,128]{2,1,0:T(8,128)(2,1)S(1)}, f32[32,64,128]{2,1,0:T(8,128)S(1)}, f32[16,1,256]{2,1,0:T(1,128)S(1)}) custom-call(f32[1]{0:T(128)} %bitcast.1.slope_ref, bf16[32,64,128]{2,1,0:T(8,128)(2,1)S(1)} %get-tuple-element.133.query_doc_ref, ...), custom_call_target="tpu_custom_call" | custom-call | bytes 221400000 | tf_op jit(solution)/shard_map/attention_forward/pallas_call | solution.py:705
  288.2 5.3 fusion.2
  296.9 21.5 %all-gather.15.cloned.1.call-done = bf16[1,3072,768]{2,1,0:T(8,128)(2,1)} async-done(((bf16[1,96,768]{2,1,0:T(8,128)(2,1)}), bf16[1,3072,768]{2,1,0:T(8,128)(2,1)}) %all-gather.15.cloned.1.call-update) | async-done | bytes 4718608 | tf_op jit(solution)/shard_map/all_gather | solution.py:1089
  318.5 3.9 fusion.110
  324.9 3.9 convolution_convert_fusion.5
  330.1 3.5 fusion.17
  333.6 5.7 convolution_convert_fusion.1
  339.4 2.9 multiply_reduce_fusion.4
  346.9 126.9 %attention_backward.2 = (bf16[24,192,128]{2,1,0:T(8,128)(2,1)}, f32[96,768]{1,0:T(8,128)}, f32[24,6144]{1,0:T(8,128)}, f32[24,896]{1,0:T(8,128)}) custom-call(f32[1]{0:T(128)} %bitcast.1.slope_ref, bf16[32,64,128]{2,1,0:T(8,128)(2,1)} %copy-done.4, bf16[32,64,128]{2,1,0:T(8,128)(2,1)} %copy-done.3, f32[32,64,128]{2,1,0:T(8,128)} %copy-done.9, ...), custom_call_target="tpu_custom_call" | custom-call | bytes 258300000 | tf_op jit(solution)/shard_map/attention_backward/pallas_call | solution.py:901
  476.5 3.7 multiply_reduce_fusion
  480.6 4.4 fusion.23
  485.1 3.7 convolution_convert_fusion.4
  488.9 2.9 multiply_reduce_fusion.1
  491.9 5.7 convolution_convert_fusion
  499.4 3.1 convolution_convert_fusion.3
  505.2 144.2 %attention_backward.3 = (bf16[24,192,128]{2,1,0:T(8,128)(2,1)}, f32[96,768]{1,0:T(8,128)}, f32[24,6144]{1,0:T(8,128)}, f32[24,896]{1,0:T(8,128)}) custom-call(f32[1]{0:T(128)} %bitcast.1.slope_ref, bf16[32,64,128]{2,1,0:T(8,128)(2,1)} %copy-done.4, bf16[32,64,128]{2,1,0:T(8,128)(2,1)} %copy-done.3, f32[32,64,128]{2,1,0:T(8,128)} %copy-done.8, ...), custom_call_target="tpu_custom_call" | custom-call | bytes 258300000 | tf_op jit(solution)/shard_map/attention_backward/pallas_call | solution.py:901
  651.9 3.2 convolution_add_fusion.2
  661.0 58.7 %scatter_grads.1 = (f32[24,2304]{1,0:T(8,128)S(1)}, f32[24,2304]{1,0:T(8,128)S(1)}) custom-call(bf16[2,4,2,2,24,2304]{5,4,3,2,1,0:T(8,128)(2,1)S(1)} %bitcast.141, bf16[2,4,2,2,24,2304]{5,4,3,2,1,0:T(8,128)(2,1)S(1)} %bitcast.140), custom_call_target="tpu_custom_call" | custom-call | bytes 110700000 | tf_op jit(solution)/shard_map/scatter_grads/pallas_call | solution.py:310
  723.1 2.8 fusion.94
  (297 shorter events, 65.6 us)
Async XLA Ops:
  7.2 198.9 %all-gather.11.cloned.1.call-start = ((), (), s32[]{:S(2)}) async-start(), calls=%async_computation.1 | async-start | bytes 1419264 | tf_op jit(solution)/shard_map/all_gather | solution.py:1089
  9.7 198.6 %all-gather.9.cloned.1.call-start = ((), (), s32[]{:S(2)}) async-start(), calls=%async_computation | async-start | bytes 3649536 | tf_op jit(solution)/shard_map/all_gather | solution.py:1089
  11.5 276.7 %all-gather.13.cloned.1.call-start = ((), (), s32[]{:S(2)}) async-start(), calls=%async_computation.2 | async-start | bytes 9732096 | tf_op jit(solution)/shard_map/all_gather | solution.py:1089
  13.6 304.9 %all-gather.15.cloned.1.call-start = ((), (), s32[]{:S(2)}) async-start(), calls=%async_computation.3 | async-start | bytes 4866048 | tf_op jit(solution)/shard_map/all_gather | solution.py:1089
  55.7 162.4 %copy-start.3 = (bf16[32,64,128]{2,1,0:T(8,128)(2,1)}, bf16[32,64,128]{2,1,0:T(8,128)(2,1)S(1)}, u32[]{:S(2)}) copy-start(bf16[32,64,128]{2,1,0:T(8,128)(2,1)S(1)} %get-tuple-element.132.key_doc_ref) | copy-start | bytes 1572868
  55.7 162.4 %copy-start.4 = (bf16[32,64,128]{2,1,0:T(8,128)(2,1)}, bf16[32,64,128]{2,1,0:T(8,128)(2,1)S(1)}, u32[]{:S(2)}) copy-start(bf16[32,64,128]{2,1,0:T(8,128)(2,1)S(1)} %get-tuple-element.133.query_doc_ref) | copy-start | bytes 1572868
  193.9 92.0 %copy-start.60 = (f32[768]{0:T(1024)}, f32[768]{0:T(1024)S(1)}, u32[]{:S(2)}) copy-start(f32[768]{0:T(1024)S(1)} %get-tuple-element.83) | copy-start | bytes 9220
  193.9 92.0 %copy-start.66 = (f32[768]{0:T(1024)}, f32[768]{0:T(1024)S(1)}, u32[]{:S(2)}) copy-start(f32[768]{0:T(1024)S(1)} %get-tuple-element.84) | copy-start | bytes 9220
  205.9 80.0 %copy-start.18 = (f32[256,768]{1,0:T(8,128)}, f32[256,768]{1,0:T(8,128)S(1)}, u32[]{:S(2)}) copy-start(f32[256,768]{1,0:T(8,128)S(1)} %get-tuple-element.137) | copy-start | bytes 2359300
  205.9 80.0 %copy-start.64 = (f32[256]{0:T(256)}, f32[256]{0:T(256)S(1)}, u32[]{:S(2)}) copy-start(f32[256]{0:T(256)S(1)} %broadcast_multiply_fusion.2) | copy-start | bytes 3076
  206.1 79.8 %copy-start.70 = (f32[256]{0:T(256)}, f32[256]{0:T(256)S(1)}, u32[]{:S(2)}) copy-start(f32[256]{0:T(256)S(1)} %fusion.77) | copy-start | bytes 3076
  346.9 129.6 %copy-start.19 = (f32[256,768]{1,0:T(8,128)S(1)}, f32[256,768]{1,0:T(8,128)}, u32[]{:S(2)}) copy-start(f32[256,768]{1,0:T(8,128)} %copy-done.18) | copy-start | bytes 2359300
  346.9 129.6 %copy-start.24 = (f32[256,768]{1,0:T(8,128)S(1)}, f32[256,768]{1,0:T(8,128)}, u32[]{:S(2)}) copy-start(f32[256,768]{1,0:T(8,128)} %copy-done.23) | copy-start | bytes 2359300
  346.9 129.6 %copy-start.61 = (f32[768]{0:T(1024)S(1)}, f32[768]{0:T(1024)}, u32[]{:S(2)}) copy-start(f32[768]{0:T(1024)} %copy-done.60) | copy-start | bytes 9220
  346.9 129.6 %copy-start.65 = (f32[256]{0:T(256)S(1)}, f32[256]{0:T(256)}, u32[]{:S(2)}) copy-start(f32[256]{0:T(256)} %copy-done.64) | copy-start | bytes 3076
  346.9 129.6 %copy-start.71 = (f32[256]{0:T(256)S(1)}, f32[256]{0:T(256)}, u32[]{:S(2)}) copy-start(f32[256]{0:T(256)} %copy-done.70) | copy-start | bytes 3076
  505.2 146.7 %copy-start.6 = (bf16[2,4,2,2,24,2304]{5,4,3,2,1,0:T(8,128)(2,1)S(1)}, bf16[2,4,2,2,24,2304]{5,4,3,2,1,0:T(8,128)(2,1)}, u32[]{:S(2)}) copy-start(bf16[2,4,2,2,24,2304]{5,4,3,2,1,0:T(8,128)(2,1)} %copy-done.5) | copy-start | bytes 10616836
  661.0 58.9 %copy-start.41 = (f32[2,24,2304]{2,1,0:T(8,128)S(1)}, f32[2,24,2304]{2,1,0:T(8,128)}, u32[]{:S(2)}) copy-start(f32[2,24,2304]{2,1,0:T(8,128)} %param.23) | copy-start | bytes 1327108
  661.0 58.9 %copy-start.42 = (f32[2,24,2304]{2,1,0:T(8,128)S(1)}, f32[2,24,2304]{2,1,0:T(8,128)}, u32[]{:S(2)}) copy-start(f32[2,24,2304]{2,1,0:T(8,128)} %param.22) | copy-start | bytes 1327108
  661.0 60.3 %copy-start.38 = (f32[2,24,768]{2,1,0:T(8,128)S(1)}, f32[2,24,768]{2,1,0:T(8,128)}, u32[]{:S(2)}) copy-start(f32[2,24,768]{2,1,0:T(8,128)} %param.24) | copy-start | bytes 442372
  661.0 60.3 %copy-start.47 = (f32[1,24,768]{2,1,0:T(8,128)S(1)}, f32[1,24,768]{2,1,0:T(8,128)}, u32[]{:S(2)}) copy-start(f32[1,24,768]{2,1,0:T(8,128)} %get-tuple-element.145) | copy-start | bytes 221188
  661.0 60.3 %copy-start.48 = (f32[1,24,768]{2,1,0:T(8,128)S(1)}, f32[1,24,768]{2,1,0:T(8,128)}, u32[]{:S(2)}) copy-start(f32[1,24,768]{2,1,0:T(8,128)} %get-tuple-element.146) | copy-start | bytes 221188
  661.0 60.2 %copy-start.49 = (f32[2,24,768]{2,1,0:T(8,128)S(1)}, f32[2,24,768]{2,1,0:T(8,128)}, u32[]{:S(2)}) copy-start(f32[2,24,768]{2,1,0:T(8,128)} %param.26) | copy-start | bytes 442372
  661.0 60.2 %copy-start.50 = (f32[2,24,768]{2,1,0:T(8,128)S(1)}, f32[2,24,768]{2,1,0:T(8,128)}, u32[]{:S(2)}) copy-start(f32[2,24,768]{2,1,0:T(8,128)} %param.25) | copy-start | bytes 442372
  (75 other events, 411.3 us)
Sparse Core Ops, SparseCore 0:
  11.5 59.3 all-gather.10
  74.3 76.5 all-gather.8
  154.4 92.6 all-gather.12
  250.4 68.0 all-gather.14
